TPU v7x, 128 devices: a whole 4x4x4 slice. The times are simulated.
128 devices in a mesh: dp: 16 (over x, z_hi, core), mp: 8 (over y, z_lo).
Axes of the slice: x: 4, y: 4, z: 4 (z_hi: 2, z_lo: 2; z = z_hi * 2 + z_lo), core: 2. Of those that a mesh axis runs over, the one named last changes fastest.
Arguments:
- hidden_rows: bfloat16 [64, 64, 5120], P('dp', None, 'mp')
- cotangent: bfloat16 [64, 64, 5120], P('dp', None, 'mp'), may hold values from -6 to 6
- lengths: int32 [64], P('dp'), may hold values from 1 to 63, as said below
- rewards: int32 [64], P('dp'), may hold values from -4 to 4
- swap_rows: int32 [16, 3, 2], P('dp'), may hold values from 0 to 3, as said below
- norm_gain: float32 [5120], P('mp'), may hold values from 0.5 to 2
- up_weight: bfloat16 [5120, 16384], P('mp', 'dp'), may hold values from -6 to 6
- down_weight: bfloat16 [16384, 5120], P('dp', 'mp'), may hold values from -6 to 6
Outputs:
- block_out: bfloat16 [64, 64, 5120], P('dp', None, 'mp')
- new_up: float32 [5120, 16384], P(None, ('dp', 'mp'))
- new_down: float32 [16384, 5120], P(('dp', 'mp'))
Inputs may be any that keep to these rules, and one draw needn't show every extreme that they name: `swap_rows`: in every group and round the 2 listed slots are distinct. `lengths`: after the swaps of the first step, the rows of each group hold at most 128 live tokens together, and some group holds exactly 128.
All inputs are finite; a program needn't handle non-finite values.
Results may differ from a plain program's by a relative error of at most 0.0058.
Values may be sent and summed in bfloat16 or wider, within the bound.
A program may use at most 128 MiB of HBM per device.

v0:
```python
import math

import jax
import jax.numpy as jnp
from jax import lax
from jax.sharding import PartitionSpec as P

norm_eps = 1e-06
step_size = 4.0


def partner(block, axis, bit):
    count = lax.axis_size(axis)
    route = []
    for low in range(count):
        high = low | 1 << bit
        if high != low and high < count:
            route += [(low, high), (high, low)]
    return lax.ppermute(block, axis, route)


def unit_slope(preact):
    sigma = jax.nn.sigmoid(preact)
    return sigma * (1.0 + preact * (1.0 - sigma))


def on_device(
    hidden_rows, cotangent, lengths, rewards, swap_rows, norm_gain, up_weight, down_weight
):
    row_count, slot_len, feat_width = hidden_rows.shape
    width_all = feat_width * lax.axis_size("mp")
    units_all = up_weight.shape[1] * lax.axis_size("dp")
    root_width = math.sqrt(width_all)
    root_units = math.sqrt(units_all)
    row_block = hidden_rows
    cot_block = cotangent
    row_lengths = lengths
    row_rewards = rewards
    for bit_index in range(swap_rows.shape[1]):
        slot_list = swap_rows[0, bit_index]
        outgoing = (
            jnp.stack([row_block[slot_list], cot_block[slot_list]]),
            jnp.stack([row_lengths[slot_list], row_rewards[slot_list]]),
        )
        incoming = partner((outgoing[0], outgoing[1]), "dp", bit_index)
        row_block = row_block.at[slot_list].set(incoming[0][0])
        cot_block = cot_block.at[slot_list].set(incoming[0][1])
        row_lengths = row_lengths.at[slot_list].set(incoming[1][0])
        row_rewards = row_rewards.at[slot_list].set(incoming[1][1])
    capacity = row_count * slot_len // 2
    row_ends = jnp.cumsum(row_lengths)
    row_starts = row_ends - row_lengths
    position = jnp.arange(capacity, dtype=jnp.int32)
    owner_row = jnp.sum((position[:, None] >= row_ends[None, :]).astype(jnp.int32), axis=1)
    is_valid = position < row_ends[-1]
    owner_row = jnp.minimum(owner_row, row_count - 1)
    owner_match = jnp.arange(row_count, dtype=jnp.int32)[None, :] == owner_row[:, None]
    owner_start = jnp.sum(jnp.where(owner_match, row_starts[None, :], 0), axis=1)
    owner_reward = jnp.sum(jnp.where(owner_match, row_rewards[None, :], 0), axis=1)
    source_index = jnp.where(is_valid, owner_row * slot_len + position - owner_start, 0)
    stacked = jnp.stack([row_block, cot_block]).reshape(2, row_count * slot_len, feat_width)
    packed = jnp.take(stacked, source_index, axis=1)
    packed = jnp.where(is_valid[None, :, None], packed, jnp.zeros((), jnp.bfloat16))
    tok_hidden = packed[0]
    tok_cot = packed[1]
    as_float = tok_hidden.astype(jnp.float32)
    total_square = lax.psum(jnp.sum(as_float * as_float, axis=1), "mp")
    normed = (
        as_float * lax.rsqrt(total_square / width_all + norm_eps)[:, None] * norm_gain
    ).astype(jnp.bfloat16)
    gathered = lax.all_gather(normed, "dp", axis=0, tiled=True)
    partial_pre = jnp.dot(gathered, up_weight, preferred_element_type=jnp.float32)
    share_rows = gathered.shape[0] // lax.axis_size("mp")
    preact = lax.psum(partial_pre, "mp") / root_width
    hidden = jax.nn.silu(preact).astype(jnp.bfloat16)
    pre_share = lax.dynamic_slice_in_dim(preact, lax.axis_index("mp") * share_rows, share_rows, 0)
    block_tokens = (
        lax.psum_scatter(
            jnp.dot(hidden, down_weight, preferred_element_type=jnp.float32),
            "dp",
            scatter_dimension=0,
            tiled=True,
        )
        / root_units
    ).astype(jnp.bfloat16)
    flat_pos = jnp.arange(row_count * slot_len, dtype=jnp.int32)
    in_row = flat_pos % slot_len
    length_each = jnp.repeat(row_lengths, slot_len, total_repeat_length=row_count * slot_len)
    start_each = jnp.repeat(row_starts, slot_len, total_repeat_length=row_count * slot_len)
    is_live = in_row < length_each
    target_index = jnp.where(is_live, start_each + in_row, 0)
    block_out = jnp.where(
        is_live[:, None], jnp.take(block_tokens, target_index, axis=0), jnp.zeros((), jnp.bfloat16)
    )
    block_out = block_out.reshape(row_count, slot_len, feat_width)
    token_scale = jnp.where(is_valid, owner_reward.astype(jnp.float32) / 4.0, 0.0)
    out_grad = (tok_cot.astype(jnp.float32) * token_scale[:, None]).astype(jnp.bfloat16)
    grad_rows = lax.all_gather(out_grad, "dp", axis=0, tiled=True)
    contract_rows = (((0,), (0,)), ((), ()))
    grad_down = (
        lax.dot_general(hidden, grad_rows, contract_rows, preferred_element_type=jnp.float32)
        / root_units
    )
    back_partial = lax.dot_general(
        grad_rows, down_weight, (((1,), (1,)), ((), ())), preferred_element_type=jnp.float32
    )
    back_share = lax.psum_scatter(back_partial, "mp", scatter_dimension=0, tiled=True) / root_units
    slope_share = (back_share * unit_slope(pre_share)).astype(jnp.bfloat16)
    grad_pre = lax.all_gather(slope_share, "mp", axis=0, tiled=True)
    grad_up = (
        lax.dot_general(gathered, grad_pre, contract_rows, preferred_element_type=jnp.float32)
        / root_width
    )
    updated_up = up_weight.astype(jnp.float32) - step_size * grad_up
    updated_down = down_weight.astype(jnp.float32) - step_size * grad_down
    new_up = lax.all_to_all(updated_up, "mp", split_axis=1, concat_axis=0, tiled=True)
    new_down = lax.all_to_all(updated_down, "mp", split_axis=0, concat_axis=1, tiled=True)
    return (block_out, new_up, new_down)


def solution(mesh):
    return jax.shard_map(
        on_device,
        mesh=mesh,
        in_specs=(
            P("dp", None, "mp"),
            P("dp", None, "mp"),
            P("dp"),
            P("dp"),
            P("dp", None, None),
            P("mp"),
            P("mp", "dp"),
            P("dp", "mp"),
        ),
        out_specs=(P("dp", None, "mp"), P(None, ("dp", "mp")), P(("dp", "mp"), None)),
        check_vma=False,
    )
```

profile of v0, /device:TPU:0, one launch (start us, length us, event | category | flops | bytes accessed | tf_op | source)
XLA Modules:
  0.0 925.5 jit_solution(4340518758671401713)
XLA Ops:
  7.2 0.7 copy.54
  7.9 0.7 copy.55
  8.5 1.0 copy.52
  9.5 1.0 copy.53
  10.5 1.0 slice_reduce_fusion
  17.2 4.0 collective-permute-start.1
  21.2 1.5 collective-permute-done.1
  25.2 1.6 collective-permute-start.2
  26.8 2.1 collective-permute-done.2
  33.5 3.6 collective-permute-start.4
  37.2 0.7 fusion.9
  37.8 4.9 collective-permute-done.4
  45.2 1.6 collective-permute-start.5
  46.8 0.7 compare_and_fusion.1
  47.4 4.9 collective-permute-done.5
  54.7 1.5 pad_maximum_fusion
  56.2 1.3 gather_fusion.12
  57.5 0.8 fusion.4
  58.9 19.7 %psum.14 = f32[128]{0:T(128)S(1)} all-reduce(f32[128]{0:T(128)S(1)} %fusion.1), channel_id=1, replica_groups=mesh['dp'=16,'mp'=8] {'mp'}, use_global_device_ids=true, to_apply=%region_15.17 | all-reduce | flops 128 | bytes 1024 | tf_op jit(solution)/shard_map/psum | solution.py:67
  78.6 0.8 fusion.3
  79.5 0.7 multiply_select_fusion
  80.1 0.8 fusion
  80.9 48.3 %all-gather.4.cloned.1.call-done = bf16[2048,640]{1,0:T(8,128)(2,1)} async-done(((bf16[128,640]{1,0:T(8,128)(2,1)}), bf16[2048,640]{1,0:T(8,128)(2,1)}) %all-gather.4.cloned.1.call-update) | async-done | bytes 2621456 | tf_op jit(solution)/shard_map/all_gather | solution.py:71
  129.3 8.8 fusion.12
  138.3 43.0 %all-gather.6.cloned.1.call-done = bf16[2048,640]{1,0:T(8,128)(2,1)} async-done(((bf16[128,640]{1,0:T(8,128)(2,1)}), bf16[2048,640]{1,0:T(8,128)(2,1)}) %all-gather.6.cloned.1.call-update) | async-done | bytes 2621456 | tf_op jit(solution)/shard_map/all_gather | solution.py:98
  181.3 7.5 fusion.14
  188.8 333.3 %all-reduce.2.cloned.1.call-done = f32[2048,1024]{1,0:T(8,128)} async-done(((f32[2048,1024]{1,0:T(8,128)}), f32[2048,1024]{1,0:T(8,128)}) %all-reduce.2.cloned.1.call-update) | async-done | bytes 8388624 | tf_op jit(solution)/shard_map/psum | solution.py:74
  522.1 8.4 broadcast_multiply_fusion
  530.5 168.3 %reduce-scatter.5.cloned.1.call-done = f32[256,1024]{1,0:T(8,128)} async-done(((f32[2048,1024]{1,0:T(8,128)}), f32[256,1024]{1,0:T(8,128)}) %reduce-scatter.5.cloned.1.call-update) | async-done | bytes 1048592 | tf_op jit(solution)/shard_map/reduce_scatter | solution.py:107
  698.8 2.8 multiply_convert_fusion.1
  701.7 7.9 fusion.13
  709.6 1.7 copy-done.1
  711.4 7.6 multiply_subtract_fusion
  719.0 4.5 all-to-all-start.1
  723.4 97.2 %all-gather.8.cloned.1.call-done = bf16[2048,1024]{1,0:T(8,128)(2,1)} async-done(((bf16[256,1024]{1,0:T(8,128)(2,1)}), bf16[2048,1024]{1,0:T(8,128)(2,1)}) %all-gather.8.cloned.1.call-update) | async-done | bytes 4194320 | tf_op jit(solution)/shard_map/all_gather | solution.py:109
  820.6 6.3 subtract_bitcast_fusion
  826.9 1.7 copy.33
  828.6 1.5 copy-done
  830.1 5.7 all-to-all-start
  835.8 0.6 fusion.11
  836.5 0.7 fusion.10
  837.1 5.2 compare_and_fusion.2
  842.5 3.7 copy.28
  846.1 67.9 %reduce-scatter.3.cloned.1.call-done = f32[128,640]{1,0:T(8,128)} async-done(((f32[2048,640]{1,0:T(8,128)}), f32[128,640]{1,0:T(8,128)}) %reduce-scatter.3.cloned.1.call-update) | async-done | bytes 327696 | tf_op jit(solution)/shard_map/reduce_scatter | solution.py:78
  914.1 1.0 multiply_convert_fusion.2
  915.1 1.2 gather_fusion.13
  916.3 0.9 select_select_fusion
  917.2 1.5 copy.56
  (84 shorter events, 18.8 us)
Async XLA Ops:
  7.2 122.1 %all-gather.4.cloned.1.call-start = ((), (), s32[]{:S(2)}) async-start(), calls=%async_computation.4 | async-start | bytes 2785280 | tf_op jit(solution)/shard_map/all_gather | solution.py:71
  12.8 1.9 collective-permute-start
  14.1 16.8 %collective-permute-start.3 = (bf16[2,2,64,640]{3,2,1,0:T(8,128)(2,1)S(1)}, bf16[2,2,64,640]{3,2,1,0:T(8,128)(2,1)S(1)}, u32[]{:S(2)}, u32[]{:S(2)}) collective-permute-start(bf16[2,2,64,640]{3,2,1,0:T(8,128)(2,1)S(1)} %pad_maximum_fusion.1), channel_id=1, source_target_pairs={{0,8},{8,0},{16,24},{24,16},{32,40},{40,32},{48,56},{56,48},{64,72... | collective-permute-start | bytes 983048 | tf_op jit(solution)/shard_map/ppermute | solution.py:19
  17.2 5.6 collective-permute-start.1
  25.2 3.6 collective-permute-start.2
  33.5 9.2 collective-permute-start.4
  45.2 7.2 collective-permute-start.5
  54.7 23.9 %copy-start.3 = (f32[640]{0:T(1024)S(1)}, f32[640]{0:T(1024)}, u32[]{:S(2)}) copy-start(f32[640]{0:T(1024)} %param.19) | copy-start | bytes 7684
  79.4 101.9 %all-gather.6.cloned.1.call-start = ((), (), s32[]{:S(2)}) async-start(), calls=%async_computation.7 | async-start | bytes 2785280 | tf_op jit(solution)/shard_map/all_gather | solution.py:98
  80.9 441.2 %all-reduce.2.cloned.1.call-start = ((), (), s32[]{:S(2)}) async-start(), calls=%async_computation.5 | async-start | bytes 16777216 | tf_op jit(solution)/shard_map/psum | solution.py:74
  138.0 43.3 %copy-start.2 = (bf16[1024,640]{1,0:T(8,128)(2,1)S(1)}, bf16[1024,640]{1,0:T(8,128)(2,1)}, u32[]{:S(2)}) copy-start(bf16[1024,640]{1,0:T(8,128)(2,1)} %param.21) | copy-start | bytes 3932164
  138.1 560.7 %reduce-scatter.5.cloned.1.call-start = ((), (), s32[]{:S(2)}) async-start(), calls=%async_computation.8 | async-start | bytes 9437184 | tf_op jit(solution)/shard_map/reduce_scatter | solution.py:107
  188.8 631.8 %all-gather.8.cloned.1.call-start = ((), (), s32[]{:S(2)}) async-start(), calls=%async_computation.9 | async-start | bytes 4718592 | tf_op jit(solution)/shard_map/all_gather | solution.py:109
  701.6 212.5 %reduce-scatter.3.cloned.1.call-start = ((), (), s32[]{:S(2)}) async-start(), calls=%async_computation.6 | async-start | bytes 5570560 | tf_op jit(solution)/shard_map/reduce_scatter | solution.py:78
  709.6 1.7 copy-start.1
  719.0 109.6 %all-to-all-start.1 = ((f32[8,128,640]{2,1,0:T(8,128)}), f32[8,128,640]{2,1,0:T(8,128)S(1)}, u32[]{:S(2)}, u32[]{:S(2)}) async-start(f32[8,128,640]{2,1,0:T(8,128)} %bitcast.137), calls=%async_computation.3 | async-start | bytes 5242880 | tf_op jit(solution)/shard_map/all_to_all | solution.py:117
  828.6 1.5 copy-start
  828.6 8.6 copy-start.4
  830.1 87.1 %all-to-all-start = ((f32[640,8,128]{2,0,1:T(8,128)}), f32[640,8,128]{2,0,1:T(8,128)S(1)}, u32[]{:S(2)}, u32[]{:S(2)}) async-start(f32[640,8,128]{2,0,1:T(8,128)} %bitcast.121), calls=%async_computation.2 | async-start | bytes 5242880 | tf_op jit(solution)/shard_map/all_to_all | solution.py:116
Sparse Core Ops, SparseCore 0:
  79.5 49.7 all-gather.3
  132.3 49.0 all-gather.5
  183.8 338.2 all-reduce.1
  524.4 174.3 reduce-scatter.4
  701.7 118.8 all-gather.7
  824.5 89.5 reduce-scatter.2
where the time goes:
time: 926 us; the launch traced here: 925 us
  waiting for transfers between devices  772 us (83%)
  matrix products  38.1 us (4%)
  local copies, waits for them, and re-layouts  34.5 us (4%)
  other arithmetic  25.2 us (3%)
  starting transfers between devices  22.1 us (2%)
  blocking collectives  19.7 us (2%)
  between operations  14.5 us (2%)
    psum x1, waiting for transfers between devices, on_device(): preact = lax.psum(partial_pre, 'mp') / root_width  333 us
    reduce_scatter x1, waiting for transfers between devices, on_device(): lax.psum_scatter(back_partial, 'mp', scatter_dimension=0, tiled=True)  168 us
    all_gather x1, waiting for transfers between devices, on_device(): grad_pre = lax.all_gather(slope_share, 'mp', axis=0, tiled=True)  97.2 us
    reduce_scatter x1, waiting for transfers between devices, on_device(): lax.psum_scatter(jnp.dot(hidden, down_weight, preferred_element_type=jnp....  67.9 us
    all_gather x1, waiting for transfers between devices, on_device(): gathered = lax.all_gather(normed, 'dp', axis=0, tiled=True)  48.3 us
    all_gather x1, waiting for transfers between devices, on_device(): grad_rows = lax.all_gather(out_grad, 'dp', axis=0, tiled=True)  43 us
    psum x1, blocking collectives, on_device(): total_square = lax.psum(jnp.sum(as_float * as_float, axis=1), 'mp')  19.7 us
  transfers between devices with their start and end apart: 14, of which 10 were waited for; matrix products, arithmetic and copies ran while one was open for 8% of the time, Pallas kernels for 0%

commit v1 on v0

v1 whole, which is shorter than its diff:
```python
import math

import jax
import jax.numpy as jnp
from jax import lax
from jax.experimental import pallas as pl
from jax.experimental.pallas import tpu as pltpu
from jax.sharding import PartitionSpec as P

norm_eps = 1e-06
step_size = 4.0
MESH = pl.DeviceIdType.MESH

CAP = 128
ORDERS = (("x", "y", "z"), ("y", "z", "x"), ("z", "x", "y"))
PARTS = ((0, 48), (48, 48), (96, 32))
OFFSETS = (1, 3, 2)


def place():
    i = lax.axis_index("dp")
    j = lax.axis_index("mp")
    return {
        "x": i // 4,
        "y": j // 2,
        "z": ((i // 2) % 2) * 2 + j % 2,
        "c": i % 2,
    }


def device(at):
    z = at["z"]
    return ((at["x"] * 2 + z // 2) * 2 + at["c"], at["y"] * 2 + z % 2)


def shifted(at, axis, step):
    count = 2 if axis == "c" else 4
    return {**at, axis: (at[axis] + step) % count}


def spans(sel):
    def plain(s):
        if isinstance(s, tuple):
            return pl.ds(2 * s[1], 2)
        return pl.ds(0, 4) if s is None else pl.ds(s, 1)

    z = sel["z"]
    if z is None:
        z_lo, z_hi = pl.ds(0, 2), pl.ds(0, 2)
    elif isinstance(z, tuple):
        z_lo, z_hi = pl.ds(0, 2), pl.ds(z[1], 1)
    else:
        z_lo, z_hi = pl.ds(z % 2, 1), pl.ds(z // 2, 1)
    return (plain(sel["y"]), z_lo, plain(sel["x"]), z_hi)


def remote(src, dst, send, recv, at):
    return pltpu.make_async_remote_copy(
        src_ref=src,
        dst_ref=dst,
        send_sem=send,
        recv_sem=recv,
        device_id=device(at),
        device_id_type=MESH,
    )


def enter(peers):
    barrier = pltpu.get_barrier_semaphore()
    for at in peers:
        pl.semaphore_signal(barrier, inc=1, device_id=device(at), device_id_type=MESH)
    pl.semaphore_wait(barrier, len(peers))


def axis_peers(at):
    return [shifted(at, axis, k) for axis in "xyz" for k in OFFSETS]


def row_mask(meta, slot, slot_len):
    length = meta[slot, 0:1, 0:1]
    start = jnp.zeros((1, 1), jnp.int32)
    for before in range(slot):
        start = start + meta[before, 0:1, 0:1]
    token = lax.broadcasted_iota(jnp.int32, (CAP, slot_len), 0)
    spot = lax.broadcasted_iota(jnp.int32, (CAP, slot_len), 1)
    hit = jnp.logical_and(token == spot + start, spot < length)
    return jnp.where(hit, 1.0, 0.0).astype(jnp.bfloat16)


def gather_kernel(
    hid, cot, gain, lens, rew, swp, up, dn,
    g_norm, g_out, w_up, w_dn, meta_out,
    rows, out_rows, in_rows, meta, out_meta, in_meta, squares, packed,
    sq_send, sq_recv, swap_send, swap_recv, meta_send, meta_recv,
    up_send, up_recv, dn_send, dn_recv, local_sem, core_send, core_recv,
    s1_send, s1_recv, s2_send, s2_recv, s3_send, s3_recv,
):
    at = place()
    row_count, slot_len, width = hid.shape
    units = 128
    mp_peers = [
        shifted(shifted(at, "y", dy), "z", 0) if not dz else {**shifted(at, "y", dy), "z": (at["z"] // 2) * 2 + 1 - at["z"] % 2}
        for dy in range(4) for dz in range(2) if dy or dz
    ]
    diagonal = [p for n, p in enumerate(mp_peers) if n in (2, 4, 6)]
    core = shifted(at, "c", 1)
    enter(axis_peers(at) + diagonal + [core])

    flat = hid[...].reshape(row_count * slot_len, width).astype(jnp.float32)
    squares[7] = lax.dot_general(
        jnp.ones((8, width), jnp.float32), flat * flat, (((1,), (1,)), ((), ())),
        precision=lax.Precision.HIGHEST, preferred_element_type=jnp.float32,
    )
    sq_copies = []
    for n, peer in enumerate(mp_peers):
        copy = remote(squares.at[7], squares.at[n], sq_send.at[n], sq_recv.at[n], peer)
        copy.start()
        sq_copies.append(copy)

    for s in range(row_count):
        scale = rew[s].astype(jnp.float32) / 4.0
        rows[s, 1] = (cot[s].astype(jnp.float32) * scale).astype(jnp.bfloat16)
        meta[s] = jnp.full((8, 128), lens[s], jnp.int32)

    total = squares[7]
    for n, copy in enumerate(sq_copies):
        copy.wait()
        total = total + squares[n]
    factor = lax.rsqrt(total / (8 * width) + norm_eps)
    column = jnp.transpose(factor)[:, 0:1]
    normed = (flat * column * gain[...]).astype(jnp.bfloat16)
    for s in range(row_count):
        rows[s, 0] = normed[s * slot_len : (s + 1) * slot_len]

    j_me = at["y"] * 2 + at["z"] % 2
    own_units = pl.ds(pl.multiple_of(at["c"] * units, units), units)
    weight_copies = []
    for n, peer in enumerate(mp_peers):
        j_to = peer["y"] * 2 + peer["z"] % 2
        cut = pl.ds(pl.multiple_of(j_to * units, units), units)
        weight_copies.append(
            remote(up.at[:, cut], w_up.at[j_me, :, own_units], up_send.at[n], up_recv.at[n], peer)
        )
        weight_copies.append(
            remote(dn.at[cut], w_dn.at[j_me, own_units], dn_send.at[n], dn_recv.at[n], peer)
        )
    cut = pl.ds(pl.multiple_of(j_me * units, units), units)
    weight_copies.append(
        pltpu.make_async_copy(up.at[:, cut], w_up.at[j_me, :, own_units], local_sem.at[0])
    )
    weight_copies.append(
        pltpu.make_async_copy(dn.at[cut], w_dn.at[j_me, own_units], local_sem.at[1])
    )
    for copy in weight_copies:
        copy.start()

    partners = (core, shifted(at, "z", 2), {**at, "x": (at["x"] // 2) * 2 + 1 - at["x"] % 2})
    for r, peer in enumerate(partners):
        first, second = swp[r, 0], swp[r, 1]
        out_rows[r, 0] = rows[first]
        out_rows[r, 1] = rows[second]
        out_meta[r, 0] = meta[first]
        out_meta[r, 1] = meta[second]
        row_copy = remote(out_rows.at[r], in_rows.at[r], swap_send.at[r], swap_recv.at[r], peer)
        meta_copy = remote(out_meta.at[r], in_meta.at[r], meta_send.at[r], meta_recv.at[r], peer)
        meta_copy.start()
        row_copy.start()
        meta_copy.wait()
        row_copy.wait()
        for s in range(row_count):
            is_first, is_second = first == s, second == s
            rows[s] = jnp.where(is_first, in_rows[r, 0], jnp.where(is_second, in_rows[r, 1], rows[s]))
            meta[s] = jnp.where(is_first, in_meta[r, 0], jnp.where(is_second, in_meta[r, 1], meta[s]))
    meta_out[...] = meta[...]

    masks = [row_mask(meta, s, slot_len) for s in range(row_count)]
    for a in range(2):
        acc = jnp.zeros((CAP, width), jnp.float32)
        for s in range(row_count):
            acc = acc + jnp.dot(masks[s], rows[s, a], preferred_element_type=jnp.float32)
        packed[a, 0, 0, 0, 0] = acc.astype(jnp.bfloat16)

    here = spans({k: at[k] for k in "xyz"})
    bufs = (g_norm, g_out)
    own = []
    for a in range(2):
        copy = pltpu.make_async_copy(packed.at[a], bufs[a].at[here], local_sem.at[2 + a])
        copy.start()
        own.append(copy)
    first_copies = {}
    for a in range(2):
        for p, (r0, nr) in enumerate(PARTS):
            for k, step in enumerate(OFFSETS):
                row = pl.ds(r0, nr)
                copy = remote(
                    packed.at[a, :, :, :, :, row], bufs[a].at[here + (row,)],
                    s1_send.at[a, p, k], s1_recv.at[a, p, k], shifted(at, ORDERS[p][0], step),
                )
                copy.start()
                first_copies[a, p, k] = copy
    second_copies = {}
    for a in range(2):
        own[a].wait()
        for p, (r0, nr) in enumerate(PARTS):
            for k in range(3):
                first_copies[a, p, k].wait()
            one, two, three = ORDERS[p]
            piece = bufs[a].at[spans({one: None, two: at[two], three: at[three]}) + (pl.ds(r0, nr),)]
            for k, step in enumerate(OFFSETS):
                copy = remote(
                    piece, piece, s2_send.at[a, p, k], s2_recv.at[a, p, k], shifted(at, two, step)
                )
                copy.start()
                second_copies[a, p, k] = copy
    third_copies = {}
    for a in range(2):
        for p, (r0, nr) in enumerate(PARTS):
            for k in range(3):
                second_copies[a, p, k].wait()
            one, two, three = ORDERS[p]
            piece = bufs[a].at[spans({one: None, two: None, three: at[three]}) + (pl.ds(r0, nr),)]
            for k, step in enumerate((1, 3)):
                copy = remote(
                    piece, piece, s3_send.at[a, p, k], s3_recv.at[a, p, k], shifted(at, three, step)
                )
                copy.start()
                third_copies[a, p, k] = copy
    for copy in weight_copies:
        copy.wait()
    core_copies = []
    for n, (buf, where) in enumerate(((w_up, (slice(None), slice(None), own_units)), (w_dn, (slice(None), own_units)))):
        copy = remote(buf.at[where], buf.at[where], core_send.at[n], core_recv.at[n], core)
        copy.start()
        core_copies.append(copy)
    for a in range(2):
        for p, (r0, nr) in enumerate(PARTS):
            one, two, three = ORDERS[p]
            for k, step in enumerate((1, 3)):
                third_copies[a, p, k].wait()
                origin = (at[three] - step) % 4
                piece = bufs[a].at[spans({one: ("half", k), two: None, three: origin}) + (pl.ds(r0, nr),)]
                copy = remote(
                    piece, piece, s3_send.at[a, p, 2 + k], s3_recv.at[a, p, 2 + k], shifted(at, three, step)
                )
                copy.start()
                third_copies[a, p, 2 + k] = copy
    for a in range(2):
        for p in range(3):
            for k in range(2):
                third_copies[a, p, 2 + k].wait()
    for copy in core_copies:
        copy.wait()


def gather_all(hid, cot, gain, lens, rew, swp, up, dn):
    row_count, slot_len, width = hid.shape
    bf16 = jnp.bfloat16
    blocks = (4, 2, 4, 2, CAP, width)
    dma = pltpu.SemaphoreType.DMA
    vmem = pl.BlockSpec(memory_space=pltpu.VMEM)
    smem = pl.BlockSpec(memory_space=pltpu.SMEM)
    hbm = pl.BlockSpec(memory_space=pl.ANY)
    return pl.pallas_call(
        gather_kernel,
        out_shape=(
            jax.ShapeDtypeStruct(blocks, bf16),
            jax.ShapeDtypeStruct(blocks, bf16),
            jax.ShapeDtypeStruct((8, width, 256), bf16),
            jax.ShapeDtypeStruct((8, 256, width), bf16),
            jax.ShapeDtypeStruct((row_count, 8, 128), jnp.int32),
        ),
        in_specs=[vmem, vmem, vmem, smem, smem, smem, hbm, hbm],
        out_specs=(hbm, hbm, hbm, hbm, vmem),
        scratch_shapes=[
            pltpu.VMEM((row_count, 2, slot_len, width), bf16),
            pltpu.VMEM((3, 2, 2, slot_len, width), bf16),
            pltpu.VMEM((3, 2, 2, slot_len, width), bf16),
            pltpu.VMEM((row_count, 8, 128), jnp.int32),
            pltpu.VMEM((3, 2, 8, 128), jnp.int32),
            pltpu.VMEM((3, 2, 8, 128), jnp.int32),
            pltpu.VMEM((8, 8, row_count * slot_len), jnp.float32),
            pltpu.VMEM((2, 1, 1, 1, 1, CAP, width), bf16),
            dma((7,)), dma((7,)), dma((3,)), dma((3,)), dma((3,)), dma((3,)),
            dma((7,)), dma((7,)), dma((7,)), dma((7,)), dma((4,)), dma((2,)), dma((2,)),
            dma((2, 3, 3)), dma((2, 3, 3)), dma((2, 3, 3)), dma((2, 3, 3)),
            dma((2, 3, 4)), dma((2, 3, 4)),
        ],
        compiler_params=pltpu.CompilerParams(
            collective_id=1, has_side_effects=True, vmem_limit_bytes=32 << 20
        ),
        name="gather_all",
    )(hid, cot, gain, lens, rew, swp, up, dn)


def unit_slope(preact):
    sigma = 1.0 / (1.0 + jnp.exp(-preact))
    return sigma * (1.0 + preact * (1.0 - sigma))


def forward_kernel(root_width, g, w, preact, hidden, acc):
    j = pl.program_id(0)

    @pl.when(j == 0)
    def _():
        acc[...] = jnp.zeros_like(acc)

    acc[...] += jnp.dot(g[0], w[0], preferred_element_type=jnp.float32)

    @pl.when(j == 7)
    def _():
        value = acc[...] / root_width
        preact[...] = value
        hidden[...] = (value / (1.0 + jnp.exp(-value))).astype(jnp.bfloat16)


def middle_kernel(root_units, g, w, preact, hidden, block, grad_dn, grad_pre, acc):
    j = pl.program_id(0)
    c = lax.axis_index("dp") % 2

    @pl.when(j == 0)
    def _():
        acc[...] = jnp.zeros_like(acc)

    block[0] = jnp.dot(hidden[...], w[0], preferred_element_type=jnp.float32).astype(jnp.bfloat16)
    acc[...] += lax.dot_general(
        g[0], w[0], (((1,), (1,)), ((), ())), preferred_element_type=jnp.float32
    )
    grad = lax.dot_general(
        hidden[...], g[0], (((0,), (0,)), ((), ())), preferred_element_type=jnp.float32
    ) * (step_size / root_units)
    for h in range(2):
        base = jnp.where(c == h, w[0, h * 128 : (h + 1) * 128].astype(jnp.float32), 0.0)
        grad_dn[h] = base - grad[h * 128 : (h + 1) * 128]

    @pl.when(j == 7)
    def _():
        grad_pre[...] = (acc[...] / root_units * unit_slope(preact[...])).astype(jnp.bfloat16)


def up_kernel(root_width, g, w, grad_pre, grad_up):
    c = lax.axis_index("dp") % 2
    grad = lax.dot_general(
        g[0], grad_pre[...], (((0,), (0,)), ((), ())), preferred_element_type=jnp.float32
    ) * (step_size / root_width)
    for h in range(2):
        base = jnp.where(c == h, w[0, :, h * 128 : (h + 1) * 128].astype(jnp.float32), 0.0)
        grad_up[h] = base - grad[:, h * 128 : (h + 1) * 128]


def local_math(g_norm, g_out, w_up, w_dn, root_width, root_units):
    width = g_norm.shape[-1]
    tokens = 8 * CAP
    g_norm = g_norm.reshape(8, tokens, width)
    g_out = g_out.reshape(8, tokens, width)
    f32, bf16 = jnp.float32, jnp.bfloat16
    g_spec = pl.BlockSpec((1, tokens, width), lambda j: (j, 0, 0))
    wu_spec = pl.BlockSpec((1, width, 256), lambda j: (j, 0, 0))
    wd_spec = pl.BlockSpec((1, 256, width), lambda j: (j, 0, 0))
    whole = pl.BlockSpec((tokens, 256), lambda j: (0, 0))
    params = pltpu.CompilerParams(vmem_limit_bytes=48 << 20)

    def bind(fn, *args):
        return lambda *refs: fn(*args, *refs)

    preact, hidden = pl.pallas_call(
        bind(forward_kernel, root_width),
        grid=(8,),
        in_specs=[g_spec, wu_spec],
        out_specs=(whole, whole),
        out_shape=(
            jax.ShapeDtypeStruct((tokens, 256), f32),
            jax.ShapeDtypeStruct((tokens, 256), bf16),
        ),
        scratch_shapes=[pltpu.VMEM((tokens, 256), f32)],
        compiler_params=params,
        name="forward",
    )(g_norm, w_up)
    block, grad_dn, grad_pre = pl.pallas_call(
        bind(middle_kernel, root_units),
        grid=(8,),
        in_specs=[g_spec, wd_spec, whole, whole],
        out_specs=(
            g_spec,
            pl.BlockSpec((2, 128, width), lambda j: (0, 0, j)),
            whole,
        ),
        out_shape=(
            jax.ShapeDtypeStruct((8, tokens, width), bf16),
            jax.ShapeDtypeStruct((2, 128, 8 * width), f32),
            jax.ShapeDtypeStruct((tokens, 256), bf16),
        ),
        scratch_shapes=[pltpu.VMEM((tokens, 256), f32)],
        compiler_params=params,
        name="middle",
    )(g_out, w_dn, preact, hidden)
    grad_up = pl.pallas_call(
        bind(up_kernel, root_width),
        grid=(8,),
        in_specs=[g_spec, wu_spec, whole],
        out_specs=pl.BlockSpec((2, width, 128), lambda j: (0, j, 0)),
        out_shape=jax.ShapeDtypeStruct((2, 8 * width, 128), f32),
        compiler_params=params,
        name="up_grad",
    )(g_norm, w_up, grad_pre)
    return block.reshape(4, 2, 4, 2, CAP, width), grad_dn, grad_up


def sizes(sel, nr, width):
    def plain(s):
        return 2 if isinstance(s, tuple) else (4 if s is None else 1)

    z = sel["z"]
    z_dims = (2, 2) if z is None else ((2, 1) if isinstance(z, tuple) else (1, 1))
    return (plain(sel["y"]), z_dims[0], plain(sel["x"]), z_dims[1], nr, width)


def lead(q, dims):
    d = q % dims[3]
    q = q // dims[3]
    c = q % dims[2]
    q = q // dims[2]
    b = q % dims[1]
    return (q // dims[1], b, c, d)


def scatter_kernel(root_units, part, meta, out, *refs):
    at = place()
    row_count, slot_len, width = out.shape
    half_bufs, full_bufs, two_bufs, one_bufs = refs[0:3], refs[3:6], refs[6:9], refs[9:12]
    tokens = refs[12]
    h_send, h_recv, f_send, f_recv, t_send, t_recv, o_send, o_recv = refs[13:]
    enter(axis_peers(at))
    count = lambda dims: dims[0] * dims[1] * dims[2] * dims[3]

    sends = {}
    for p, (r0, nr) in enumerate(PARTS):
        one, two, three = ORDERS[p]
        row = pl.ds(r0, nr)
        for k, step in enumerate((1, 3)):
            src = part.at[spans({one: (at[one] + 2) % 4, two: ("half", k), three: None}) + (row,)]
            sends[p, k] = remote(
                src, half_bufs[p].at[k], h_send.at[p, k], h_recv.at[p, k], shifted(at, one, step)
            )
            sends[p, k].start()
        for k, step in enumerate((1, 3)):
            other = 1 - k
            src = part.at[spans({one: (at[one] + step) % 4, two: ("half", other), three: None}) + (row,)]
            dst = full_bufs[p].at[(k,) + spans({one: 0, two: ("half", other), three: None})]
            sends[p, 2 + k] = remote(
                src, dst, f_send.at[p, k, 0], f_recv.at[p, k, 0], shifted(at, one, step)
            )
            sends[p, 2 + k].start()
    for p, (r0, nr) in enumerate(PARTS):
        one, two, three = ORDERS[p]
        for k, step in enumerate((1, 3)):
            sends[p, k].wait()
            sel = {one: 0, two: ("half", k), three: None}
            dims = sizes(sel, nr, width)[:4]
            base = {one: (at[one] + step) % 4, two: ("half", k), three: None}
            starts = [s.start for s in spans(base)]

            def add(q, carry, p=p, k=k, dims=dims, starts=starts, r0=r0, nr=nr):
                ix = lead(q, dims)
                there = tuple(s + i for s, i in zip(starts, ix))
                half_bufs[p][(k,) + ix] = half_bufs[p][(k,) + ix] + part[there + (pl.ds(r0, nr),)]
                return carry

            lax.fori_loop(0, count(dims), add, 0)
            dst = full_bufs[p].at[(k,) + spans(sel)]
            sends[p, 4 + k] = remote(
                half_bufs[p].at[k], dst, f_send.at[p, k, 1], f_recv.at[p, k, 1], shifted(at, one, step)
            )
            sends[p, 4 + k].start()
    for p, (r0, nr) in enumerate(PARTS):
        one, two, three = ORDERS[p]
        for n in (2, 3, 4, 5):
            sends[p, n].wait()
        dims = sizes({one: 0, two: None, three: None}, nr, width)[:4]
        starts = [s.start for s in spans({one: at[one], two: None, three: None})]

        def add(q, carry, p=p, dims=dims, starts=starts, r0=r0, nr=nr):
            ix = lead(q, dims)
            there = tuple(s + i for s, i in zip(starts, ix))
            value = full_bufs[p][(0,) + ix].astype(jnp.float32) + full_bufs[p][(1,) + ix].astype(jnp.float32)
            value = value + part[there + (pl.ds(r0, nr),)].astype(jnp.float32)
            full_bufs[p][(0,) + ix] = value.astype(jnp.bfloat16)
            return carry

        lax.fori_loop(0, count(dims), add, 0)
        for k, step in enumerate(OFFSETS):
            src = full_bufs[p].at[(0,) + spans({one: 0, two: (at[two] + step) % 4, three: None})]
            sends[p, 6 + k] = remote(
                src, two_bufs[p].at[k], t_send.at[p, k], t_recv.at[p, k], shifted(at, two, step)
            )
            sends[p, 6 + k].start()
    for p, (r0, nr) in enumerate(PARTS):
        one, two, three = ORDERS[p]
        for k in range(3):
            sends[p, 6 + k].wait()
        dims = sizes({one: 0, two: 0, three: None}, nr, width)[:4]
        starts = [s.start for s in spans({one: 0, two: at[two], three: None})]
        for q in range(4):
            ix = lead(q, dims)
            there = tuple(s + i for s, i in zip(starts, ix))
            value = full_bufs[p][(0,) + there].astype(jnp.float32)
            for k in range(3):
                value = value + two_bufs[p][(k,) + ix].astype(jnp.float32)
            two_bufs[p][(0,) + ix] = value.astype(jnp.bfloat16)
        for k, step in enumerate(OFFSETS):
            src = two_bufs[p].at[(0,) + spans({one: 0, two: 0, three: (at[three] + step) % 4})]
            sends[p, 9 + k] = remote(
                src, one_bufs[p].at[k], o_send.at[p, k], o_recv.at[p, k], shifted(at, three, step)
            )
            sends[p, 9 + k].start()
    for p, (r0, nr) in enumerate(PARTS):
        one, two, three = ORDERS[p]
        for k in range(3):
            sends[p, 9 + k].wait()
        there = tuple(s.start for s in spans({one: 0, two: 0, three: at[three]}))
        value = two_bufs[p][(0,) + there].astype(jnp.float32)
        for k in range(3):
            value = value + one_bufs[p][k, 0, 0, 0, 0].astype(jnp.float32)
        tokens[pl.ds(r0, nr)] = (value / root_units).astype(jnp.bfloat16)
    for s in range(row_count):
        out[s] = lax.dot_general(
            row_mask(meta, s, slot_len), tokens[...], (((0,), (0,)), ((), ())),
            preferred_element_type=jnp.float32,
        ).astype(jnp.bfloat16)


def scatter_all(part, meta, slot_len, root_units):
    width = part.shape[-1]
    row_count = meta.shape[0]
    bf16 = jnp.bfloat16
    dma = pltpu.SemaphoreType.DMA
    vmem = pl.BlockSpec(memory_space=pltpu.VMEM)
    half, full, two_b, one_b = [], [], [], []
    for (one, two, three), (_, nr) in zip(ORDERS, PARTS):
        half.append(pltpu.VMEM((2,) + sizes({one: 0, two: ("half", 0), three: None}, nr, width), bf16))
        full.append(pltpu.VMEM((2,) + sizes({one: 0, two: None, three: None}, nr, width), bf16))
        two_b.append(pltpu.VMEM((3,) + sizes({one: 0, two: 0, three: None}, nr, width), bf16))
        one_b.append(pltpu.VMEM((3, 1, 1, 1, 1, nr, width), bf16))

    def body(*refs):
        scatter_kernel(root_units, *refs)

    return pl.pallas_call(
        body,
        out_shape=jax.ShapeDtypeStruct((row_count, slot_len, width), bf16),
        in_specs=[vmem, vmem],
        out_specs=vmem,
        scratch_shapes=half + full + two_b + one_b + [
            pltpu.VMEM((CAP, width), bf16),
            dma((3, 2)), dma((3, 2)), dma((3, 2, 2)), dma((3, 2, 2)),
            dma((3, 3)), dma((3, 3)), dma((3, 3)), dma((3, 3)),
        ],
        compiler_params=pltpu.CompilerParams(
            collective_id=2, has_side_effects=True, vmem_limit_bytes=48 << 20
        ),
        name="scatter_all",
    )(part, meta)


def on_device(
    hidden_rows, cotangent, lengths, rewards, swap_rows, norm_gain, up_weight, down_weight
):
    row_count, slot_len, width = hidden_rows.shape
    root_width = math.sqrt(width * lax.axis_size("mp"))
    root_units = math.sqrt(up_weight.shape[1] * lax.axis_size("dp"))
    g_norm, g_out, w_up, w_dn, meta = gather_all(
        hidden_rows, cotangent, norm_gain.reshape(1, width), lengths, rewards,
        swap_rows.reshape(3, 2), up_weight, down_weight,
    )
    part, grad_dn, grad_up = local_math(g_norm, g_out, w_up, w_dn, root_width, root_units)
    c = lax.axis_index("dp") % 2
    pairs = [(i, i ^ 1) for i in range(lax.axis_size("dp"))]
    new = []
    for both in (grad_up, grad_dn):
        mine = lax.dynamic_index_in_dim(both, c, 0, keepdims=False)
        other = lax.dynamic_index_in_dim(both, 1 - c, 0, keepdims=False)
        new.append(mine + lax.ppermute(other, "dp", pairs))
    block_out = scatter_all(part, meta, slot_len, root_units)
    return (block_out, new[0], new[1])


def solution(mesh):
    return jax.shard_map(
        on_device,
        mesh=mesh,
        in_specs=(
            P("dp", None, "mp"),
            P("dp", None, "mp"),
            P("dp"),
            P("dp"),
            P("dp", None, None),
            P("mp"),
            P("mp", "dp"),
            P("dp", "mp"),
        ),
        out_specs=(P("dp", None, "mp"), P(None, ("dp", "mp")), P(("dp", "mp"), None)),
        check_vma=False,
    )
```

time: 926 us -> 273 us (0.29)
  waiting for transfers between devices: 772 us -> 0.01 us
  Pallas kernels: 0 us -> 246 us
  matrix products: 38.1 us -> 0 us
  starting transfers between devices: 22.1 us -> 0.13 us
  blocking collectives: 19.7 us -> 0 us
  other arithmetic: 25.2 us -> 7.85 us
  local copies, waits for them, and re-layouts: 34.5 us -> 17.5 us
  between operations: 14.5 us -> 0.7 us
    psum x1 -> x0, waiting for transfers between devices: 333 us -> none  [on_device(): preact = lax.psum(partial_pre, 'mp') / root_width]
    pallas_call x0 -> x5, Pallas kernels: none -> 246 us  [the longest x1 149 us: gather_all(): pl.pallas_call(gather_kernel, out_shape=(jax.ShapeDtypeStruct(blocks, bf1...]
    reduce_scatter x2 -> x0, waiting for transfers between devices: 236 us -> none  [the longest x1 168 us: on_device(): lax.psum_scatter(back_partial, 'mp', scatter_dimension=0, tiled=True)]
    all_gather x3 -> x0, waiting for transfers between devices: 189 us -> none  [the longest x1 97.2 us: on_device(): grad_pre = lax.all_gather(slope_share, 'mp', axis=0, tiled=True)]
    dot_general x5 -> x0, matrix products: 38.1 us -> none  [the longest x1 8.76 us: on_device(): jnp.dot(gathered, up_weight, preferred_element_type=jnp.float32)]
    psum x1 -> x0, blocking collectives: 19.7 us -> none  [on_device(): total_square = lax.psum(jnp.sum(as_float * as_float, axis=1), 'mp')]
    ppermute x6 -> x2, waiting for transfers between devices: 13.4 us -> 0.01 us  [on_device(): new.append(mine + lax.ppermute(other, 'dp', pairs))]
    ppermute x6 -> x2, starting transfers between devices: 11.4 us -> 0.13 us  [on_device(): new.append(mine + lax.ppermute(other, 'dp', pairs))]
  transfers between devices with their start and end apart: 14 -> 2, of which waited for: 10 -> 0; matrix products, arithmetic and copies ran while one was open for 8% -> 2% of each run, Pallas kernels for 0% -> 22%
where the time goes in v1:
time: 273 us; the launch traced here: 272 us
  Pallas kernels  246 us (90%)
  local copies, waits for them, and re-layouts  17.5 us (6%)
  other arithmetic  7.85 us (3%)
    pallas_call x1, Pallas kernels, gather_all(): pl.pallas_call(gather_kernel, out_shape=(jax.ShapeDtypeStruct(blocks, bf1...  149 us
    pallas_call x1, Pallas kernels, scatter_all(): pl.pallas_call(body, out_shape=jax.ShapeDtypeStruct((row_count, slot_len,...  61.2 us
    pallas_call x1, Pallas kernels, local_math(): pl.pallas_call(bind(middle_kernel, root_units), grid=(8,), in_specs=[g_sp...  16.6 us
    unnamed x17, local copies, waits for them, and re-layouts  10.8 us
    pallas_call x1, Pallas kernels, local_math(): pl.pallas_call(bind(up_kernel, root_width), grid=(8,), in_specs=[g_spec,...  10 us
    pallas_call x1, Pallas kernels, local_math(): pl.pallas_call(bind(forward_kernel, root_width), grid=(8,), in_specs=[g_s...  8.9 us
    add x2, other arithmetic, on_device(): new.append(mine + lax.ppermute(other, 'dp', pairs))  7.85 us
  transfers between devices with their start and end apart: 2, of which 0 were waited for; matrix products, arithmetic and copies ran while one was open for 2% of the time, Pallas kernels for 22%

profile of v1, /device:TPU:0, one launch (start us, length us, event | category | flops | bytes accessed | tf_op | source)
XLA Modules:
  0.0 272.2 jit_solution(9059574246280424982)
XLA Ops:
  0.6 0.7 reshape.21.gain
  1.3 0.8 copy.11.swp
  2.1 0.0 copy-start.1
  2.1 1.3 copy-done.1
  3.4 0.0 copy-start.2
  3.4 1.3 copy-done.2
  4.7 0.0 copy-start.3
  4.7 1.0 copy-done.3
  5.7 0.0 copy-start.4
  5.7 1.0 copy-done.4
  6.7 0.0 copy-start.5
  6.7 0.7 copy-done.5
  7.3 0.0 copy-start.6
  7.3 0.7 copy-done.6
  8.0 149.3 %gather_all.1 = (bf16[4,2,4,2,128,640]{5,4,3,2,1,0:T(8,128)(2,1)S(1)}, bf16[4,2,4,2,128,640]{5,4,3,2,1,0:T(8,128)(2,1)}, bf16[8,640,256]{2,1,0:T(8,128)(2,1)S(1)...) custom-call(bf16[4,64,640]{2,1,0:T(8,128)(2,1)S(1)} %copy-done.3, bf16[4,64,640]{2,1,0:T(8,128)(2,1)S(1)} %copy-done.4, ...), custom_call_target="tpu_custom_call" | custom-call | tf_op jit(solution)/shard_map/gather_all/pallas_call | solution.py:263
  157.3 0.0 copy-start
  157.3 3.8 %copy-done = bf16[4,2,4,2,128,640]{5,4,3,2,1,0:T(8,128)(2,1)} copy-done((bf16[4,2,4,2,128,640]{5,4,3,2,1,0:T(8,128)(2,1)}, bf16[4,2,4,2,128,640]{5,4,3,2,1,0:T(8,128)(2,1)S(1)}, u32[]{:S(2)}) %copy-start) | copy-done | bytes 10485784
  161.2 8.9 %forward.1 = (f32[1024,256]{1,0:T(8,128)S(1)}, bf16[1024,256]{1,0:T(8,128)(2,1)S(1)}) custom-call(bf16[8,1024,640]{2,1,0:T(8,128)(2,1)} %bitcast.12, bf16[8,640,256]{2,1,0:T(8,128)(2,1)S(1)} %get-tuple-element.16.refs_1_), custom_call_target="tpu_custom_call" | custom-call | tf_op jit(solution)/shard_map/forward/pallas_call | solution.py:365
  170.1 16.6 %middle.1 = (bf16[8,1024,640]{2,1,0:T(8,128)(2,1)}, f32[2,128,5120]{2,1,0:T(8,128)}, bf16[1024,256]{1,0:T(8,128)(2,1)S(1)}) custom-call(bf16[8,1024,640]{2,1,0:T(8,128)(2,1)} %bitcast.14, bf16[8,256,640]{2,1,0:T(8,128)(2,1)S(1)} %get-tuple-element.14.refs_1_, f32[1024,256]{1,0:T(8,128)S(1)} %get-tuple-element.17.refs_2_, ...), custom_call_target="tpu_custom_call" | custom-call | tf_op jit(solution)/shard_map/middle/pallas_call | solution.py:378
  186.6 10.0 %up_grad.1 = f32[2,5120,128]{2,1,0:T(8,128)} custom-call(bf16[8,1024,640]{2,1,0:T(8,128)(2,1)} %bitcast.13, bf16[8,640,256]{2,1,0:T(8,128)(2,1)S(1)} %get-tuple-element.16.refs_1_, bf16[1024,256]{1,0:T(8,128)(2,1)S(1)} %get-tuple-element.21.refs_2_), custom_call_target="tpu_custom_call" | custom-call | tf_op jit(solution)/shard_map/up_grad/pallas_call | solution.py:396
  196.7 0.0 copy-start.7
  196.7 3.5 %dynamic-slice_bitcast_fusion.1 = f32[5120,128]{1,0:T(8,128)} fusion(f32[2,5120,128]{2,1,0:T(8,128)} %up_grad.1, s32[]{:T(128)S(6)} %select_n.19), kind=kLoop, calls=%fused_computation.3 | loop fusion | bytes 5242884 | tf_op jit(solution)/shard_map/jit(dynamic_index_in_dim)/squeeze | solution.py:580
  200.2 0.0 collective-permute-start
  200.2 0.4 copy-done.7
  200.6 1.7 dynamic-slice_bitcast_fusion
  202.3 0.1 collective-permute-start.1
  202.4 61.2 %scatter_all.1 = bf16[4,64,640]{2,1,0:T(8,128)(2,1)S(1)} custom-call(bf16[4,2,4,2,128,640]{5,4,3,2,1,0:T(8,128)(2,1)} %bitcast.15, s32[4,8,128]{2,1,0:T(8,128)S(1)} %get-tuple-element.20.refs_1_), custom_call_target="tpu_custom_call" | custom-call | tf_op jit(solution)/shard_map/scatter_all/pallas_call | solution.py:547
  263.6 0.0 collective-permute-done
  263.6 4.3 %bitcast_add_fusion.1 = f32[5120,128]{1,0:T(8,128)} fusion(f32[5120,128]{1,0:T(8,128)} %collective-permute-done, f32[2,5120,128]{2,1,0:T(8,128)} %up_grad.1, s32[]{:T(128)S(6)} %select_n.18), kind=kLoop, calls=%fused_computation.1 | loop fusion | flops 655360 | bytes 7864324 | tf_op jit(solution)/shard_map/add | solution.py:581
  267.9 0.0 collective-permute-done.1
  267.9 3.6 %bitcast_add_fusion = f32[128,5120]{1,0:T(8,128)} fusion(f32[128,5120]{1,0:T(8,128)S(1)} %collective-permute-done.1, f32[2,128,5120]{2,1,0:T(8,128)} %get-tuple-element.22, s32[]{:T(128)S(6)} %select_n.18), kind=kLoop, calls=%fused_computation | loop fusion | flops 655360 | bytes 7864324 | tf_op jit(solution)/shard_map/add | solution.py:581
  271.5 0.7 copy.13
Async XLA Ops:
  2.1 1.3 copy-start.1
  3.4 1.3 copy-start.2
  4.7 1.0 copy-start.3
  5.7 1.0 copy-start.4
  6.7 0.7 copy-start.5
  7.3 0.7 copy-start.6
  157.3 3.8 %copy-start = (bf16[4,2,4,2,128,640]{5,4,3,2,1,0:T(8,128)(2,1)}, bf16[4,2,4,2,128,640]{5,4,3,2,1,0:T(8,128)(2,1)S(1)}, u32[]{:S(2)}) copy-start(bf16[4,2,4,2,128,640]{5,4,3,2,1,0:T(8,128)(2,1)S(1)} %get-tuple-element.15) | copy-start | bytes 31457284
  196.7 3.9 %copy-start.7 = (f32[2,128,5120]{2,1,0:T(8,128)S(1)}, f32[2,128,5120]{2,1,0:T(8,128)}, u32[]{:S(2)}) copy-start(f32[2,128,5120]{2,1,0:T(8,128)} %get-tuple-element.22) | copy-start | bytes 15728644
  200.2 63.4 %collective-permute-start = (f32[5120,128]{1,0:T(8,128)}, f32[5120,128]{1,0:T(8,128)}, u32[]{:S(2)}, u32[]{:S(2)}) collective-permute-start(f32[5120,128]{1,0:T(8,128)} %dynamic-slice_bitcast_fusion.1), channel_id=1, source_target_pairs={{0,8},{8,0},{16,24},{24,16},{32,40},{40,32},{48,56},{56,48},{64,72... | collective-permute-start | bytes 7864328 | tf_op jit(solution)/shard_map/ppermute | solution.py:581
  202.3 65.6 %collective-permute-start.1 = (f32[128,5120]{1,0:T(8,128)}, f32[128,5120]{1,0:T(8,128)S(1)}, u32[]{:S(2)}, u32[]{:S(2)}) collective-permute-start(f32[128,5120]{1,0:T(8,128)} %dynamic-slice_bitcast_fusion), channel_id=1, source_target_pairs={{0,8},{8,0},{16,24},{24,16},{32,40},{40,32},{48,56},{56,48},{64,72... | collective-permute-start | bytes 7864328 | tf_op jit(solution)/shard_map/ppermute | solution.py:581

commit v2 on v0

v2 whole, which is shorter than its diff:
```python
import math

import jax
import jax.numpy as jnp
from jax import lax
from jax.experimental import pallas as pl
from jax.experimental.pallas import tpu as pltpu
from jax.sharding import PartitionSpec as P

norm_eps = 1e-06
step_size = 4.0
MESH = pl.DeviceIdType.MESH

CAP = 128
ORDERS = (("x", "y", "z"), ("y", "z", "x"), ("z", "x", "y"))
PARTS = (
    ((0, 48), (48, 48), (96, 32)),
    ((0, 32), (32, 48), (80, 48)),
    ((0, 32), (32, 48), (80, 48)),
)
OFFSETS = (1, 3, 2)


def place():
    i = lax.axis_index("dp")
    j = lax.axis_index("mp")
    return {
        "x": i // 4,
        "y": j // 2,
        "z": ((i // 2) % 2) * 2 + j % 2,
        "c": i % 2,
    }


def device(at):
    z = at["z"]
    return ((at["x"] * 2 + z // 2) * 2 + at["c"], at["y"] * 2 + z % 2)


def shifted(at, axis, step):
    count = 2 if axis == "c" else 4
    return {**at, axis: (at[axis] + step) % count}


def spans(sel):
    def plain(s):
        if isinstance(s, tuple):
            return pl.ds(2 * s[1], 2)
        return pl.ds(0, 4) if s is None else pl.ds(s, 1)

    z = sel["z"]
    if z is None:
        z_lo, z_hi = pl.ds(0, 2), pl.ds(0, 2)
    elif isinstance(z, tuple):
        z_lo, z_hi = pl.ds(0, 2), pl.ds(z[1], 1)
    else:
        z_lo, z_hi = pl.ds(z % 2, 1), pl.ds(z // 2, 1)
    return (plain(sel["y"]), z_lo, plain(sel["x"]), z_hi)


def remote(src, dst, send, recv, at):
    return pltpu.make_async_remote_copy(
        src_ref=src,
        dst_ref=dst,
        send_sem=send,
        recv_sem=recv,
        device_id=device(at),
        device_id_type=MESH,
    )


def enter(peers):
    barrier = pltpu.get_barrier_semaphore()
    for at in peers:
        pl.semaphore_signal(barrier, inc=1, device_id=device(at), device_id_type=MESH)
    pl.semaphore_wait(barrier, len(peers))


def axis_peers(at):
    return [shifted(at, axis, k) for axis in "xyz" for k in OFFSETS]


def row_mask(meta, slot, slot_len):
    length = meta[slot, 0:1, 0:1]
    start = jnp.zeros((1, 1), jnp.float32)
    for before in range(slot):
        start = start + meta[before, 0:1, 0:1]
    token = lax.broadcasted_iota(jnp.int32, (CAP, slot_len), 0).astype(jnp.float32)
    spot = lax.broadcasted_iota(jnp.int32, (CAP, slot_len), 1).astype(jnp.float32)
    return jnp.logical_and(token == spot + start, spot < length)


def sizes(sel, nr, width):
    def plain(s):
        return 2 if isinstance(s, tuple) else (4 if s is None else 1)

    z = sel["z"]
    z_dims = (2, 2) if z is None else ((2, 1) if isinstance(z, tuple) else (1, 1))
    return (plain(sel["y"]), z_dims[0], plain(sel["x"]), z_dims[1], nr, width)


def lead(q, dims):
    d = q % dims[3]
    q = q // dims[3]
    c = q % dims[2]
    q = q // dims[2]
    b = q % dims[1]
    return (q // dims[1], b, c, d)


def starts_of(sel):
    return tuple(s.start for s in spans(sel))


def moved(base, ix):
    return tuple(s + i for s, i in zip(base, ix))


def count(dims):
    return dims[0] * dims[1] * dims[2] * dims[3]


def unit_slope(preact):
    sigma = 1.0 / (1.0 + jnp.exp(-preact))
    return sigma * (1.0 + preact * (1.0 - sigma))


def step_kernel(
    root_width, root_units,
    hid, cot, gain, lens, rew, swp, up, dn,
    out, new_up, new_dn, g_norm, g_out,
    h_rows, c_rows, out_rows, in_rows, meta, out_meta, in_meta, squares, packed, masks,
    w_up, w_dn, stream, acc, hidden, turned, slope, part,
    own_up, oth_up, got_up, own_dn, oth_dn, got_dn, tokens,
    half_0, half_1, half_2, full_0, full_1, full_2,
    two_0, two_1, two_2, one_0, one_1, one_2,
    sq_send, sq_recv, swap_send, swap_recv, meta_send, meta_recv,
    up_send, up_recv, dn_send, dn_recv, local_sem, core_send, core_recv,
    s1_send, s1_recv, s2_send, s2_recv, s3_send, s3_recv,
    stream_sem, gu_send, gu_recv, gd_send, gd_recv, nu_sem, nd_sem,
    h_send, h_recv, f_send, f_recv, t_send, t_recv, o_send, o_recv,
):
    at = place()
    row_count, slot_len, width = hid.shape
    units = 128
    f32, bf16 = jnp.float32, jnp.bfloat16
    half_bufs, full_bufs = (half_0, half_1, half_2), (full_0, full_1, full_2)
    two_bufs, one_bufs = (two_0, two_1, two_2), (one_0, one_1, one_2)

    load_h = pltpu.make_async_copy(hid, h_rows, local_sem.at[4])
    load_c = pltpu.make_async_copy(cot, c_rows, local_sem.at[5])
    load_h.start()
    load_c.start()
    mp_peers = [
        {**shifted(at, "y", dy), "z": (at["z"] // 2) * 2 + (at["z"] % 2 + dz) % 2}
        for dy in range(4) for dz in range(2) if dy or dz
    ]
    diagonal = [p for n, p in enumerate(mp_peers) if n in (2, 4, 6)]
    core = shifted(at, "c", 1)
    enter(axis_peers(at) + diagonal + [core])
    partners = (core, shifted(at, "z", 2), {**at, "x": (at["x"] // 2) * 2 + 1 - at["x"] % 2})

    store = (h_rows, c_rows)

    def swap_start(r, a):
        out_rows[r, a, 0] = store[a][swp[0, r, 0]]
        out_rows[r, a, 1] = store[a][swp[0, r, 1]]
        copy = remote(
            out_rows.at[r, a], in_rows.at[r, a], swap_send.at[r, a], swap_recv.at[r, a], partners[r]
        )
        copy.start()
        return copy

    def swap_end(r, a, copy):
        copy.wait()
        first, second = swp[0, r, 0], swp[0, r, 1]
        for s in range(row_count):
            store[a][s] = jnp.where(
                first == s, in_rows[r, a, 0], jnp.where(second == s, in_rows[r, a, 1], store[a][s])
            )

    def meta_start(r):
        out_meta[r, 0] = meta[swp[0, r, 0]]
        out_meta[r, 1] = meta[swp[0, r, 1]]
        copy = remote(out_meta.at[r], in_meta.at[r], meta_send.at[r], meta_recv.at[r], partners[r])
        copy.start()
        return copy

    def meta_end(r, copy):
        copy.wait()
        first, second = swp[0, r, 0], swp[0, r, 1]
        for s in range(row_count):
            meta[s] = jnp.where(first == s, in_meta[r, 0], jnp.where(second == s, in_meta[r, 1], meta[s]))

    load_h.wait()
    move_h = swap_start(0, 0)
    flat = hid_value = h_rows[...].reshape(row_count * slot_len, width).astype(f32)
    squares[7] = lax.dot_general(
        jnp.ones((8, width), f32), flat * hid_value, (((1,), (1,)), ((), ())),
        precision=lax.Precision.HIGHEST, preferred_element_type=f32,
    )
    sq_copies = []
    for n, peer in enumerate(mp_peers):
        copy = remote(squares.at[7], squares.at[n], sq_send.at[n], sq_recv.at[n], peer)
        copy.start()
        sq_copies.append(copy)
    load_c.wait()
    move_c = swap_start(0, 1)
    swap_end(0, 0, move_h)
    move_h = swap_start(1, 0)
    total = squares[7]
    for n, copy in enumerate(sq_copies):
        copy.wait()
        total = total + squares[n]
    factor = lax.rsqrt(total / (8 * width) + norm_eps)
    for s in range(row_count):
        meta[s, 0:1] = jnp.full((1, 128), lens[s].astype(f32), f32)
        meta[s, 1:2] = jnp.full((1, 128), rew[s].astype(f32), f32)
        meta[s, 2:8] = jnp.zeros((6, 128), f32)
        meta[s, 2:3, 0:slot_len] = factor[0:1, s * slot_len : (s + 1) * slot_len]
    move_m = meta_start(0)
    swap_end(0, 1, move_c)
    move_c = swap_start(1, 1)
    meta_end(0, move_m)
    move_m = meta_start(1)

    j_me = at["y"] * 2 + at["z"] % 2
    own_units = pl.ds(pl.multiple_of(at["c"] * units, units), units)
    weight_copies = []
    for n, peer in enumerate(mp_peers):
        j_to = peer["y"] * 2 + peer["z"] % 2
        cut = pl.ds(pl.multiple_of(j_to * units, units), units)
        weight_copies.append(
            remote(up.at[:, cut], w_up.at[j_me, :, own_units], up_send.at[n], up_recv.at[n], peer)
        )
        weight_copies.append(
            remote(dn.at[cut], w_dn.at[j_me, own_units], dn_send.at[n], dn_recv.at[n], peer)
        )
    cut = pl.ds(pl.multiple_of(j_me * units, units), units)
    weight_copies.append(
        pltpu.make_async_copy(up.at[:, cut], w_up.at[j_me, :, own_units], local_sem.at[0])
    )
    weight_copies.append(
        pltpu.make_async_copy(dn.at[cut], w_dn.at[j_me, own_units], local_sem.at[1])
    )
    for copy in weight_copies:
        copy.start()

    swap_end(1, 0, move_h)
    move_h = swap_start(2, 0)
    swap_end(1, 1, move_c)
    move_c = swap_start(2, 1)
    meta_end(1, move_m)
    move_m = meta_start(2)
    meta_end(2, move_m)
    norm_scale = jnp.zeros((CAP, 1), f32)
    grad_scale = jnp.zeros((CAP, 1), f32)
    for s in range(row_count):
        hit = row_mask(meta, s, slot_len)
        masks[s] = jnp.where(hit, 1.0, 0.0).astype(bf16)
        norm_scale += jnp.sum(jnp.where(hit, meta[s, 2:3, 0:slot_len], 0.0), axis=1, keepdims=True)
        grad_scale += jnp.sum(jnp.where(hit, meta[s, 1:2, 0:slot_len], 0.0), axis=1, keepdims=True)

    def pack(a):
        picked = jnp.zeros((CAP, width), f32)
        for s in range(row_count):
            picked = picked + jnp.dot(masks[s], store[a][s], preferred_element_type=f32)
        return picked

    here = spans({k: at[k] for k in "xyz"})
    bufs = (g_norm, g_out)
    own, first_copies, second_copies, third_copies = [], {}, {}, {}

    def gather_first(a):
        copy = pltpu.make_async_copy(packed.at[a], bufs[a].at[here], local_sem.at[2 + a])
        copy.start()
        own.append(copy)
        for p, (r0, nr) in enumerate(PARTS[a]):
            for k, step in enumerate(OFFSETS):
                row = pl.ds(r0, nr)
                copy = remote(
                    packed.at[a, :, :, :, :, row], bufs[a].at[here + (row,)],
                    s1_send.at[a, p, k], s1_recv.at[a, p, k], shifted(at, ORDERS[p][0], step),
                )
                copy.start()
                first_copies[a, p, k] = copy

    def gather_second(a):
        own[a].wait()
        for p, (r0, nr) in enumerate(PARTS[a]):
            for k in range(3):
                first_copies[a, p, k].wait()
            one, two, three = ORDERS[p]
            piece = bufs[a].at[spans({one: None, two: at[two], three: at[three]}) + (pl.ds(r0, nr),)]
            for k, step in enumerate(OFFSETS):
                copy = remote(
                    piece, piece, s2_send.at[a, p, k], s2_recv.at[a, p, k], shifted(at, two, step)
                )
                copy.start()
                second_copies[a, p, k] = copy

    def gather_third(a, p):
        r0, nr = PARTS[a][p]
        for k in range(3):
            second_copies[a, p, k].wait()
        one, two, three = ORDERS[p]
        piece = bufs[a].at[spans({one: None, two: None, three: at[three]}) + (pl.ds(r0, nr),)]
        for k, step in enumerate((1, 3)):
            copy = remote(
                piece, piece, s3_send.at[a, p, k], s3_recv.at[a, p, k], shifted(at, three, step)
            )
            copy.start()
            third_copies[a, p, k] = copy

    def gather_pass_on(a, p):
        r0, nr = PARTS[a][p]
        one, two, three = ORDERS[p]
        for k, step in enumerate((1, 3)):
            third_copies[a, p, k].wait()
            origin = (at[three] - step) % 4
            piece = bufs[a].at[spans({one: ("half", k), two: None, three: origin}) + (pl.ds(r0, nr),)]
            copy = remote(
                piece, piece, s3_send.at[a, p, 2 + k], s3_recv.at[a, p, 2 + k], shifted(at, three, step)
            )
            copy.start()
            third_copies[a, p, 2 + k] = copy

    def gather_end(a):
        for p in range(3):
            for k in range(2):
                third_copies[a, p, 2 + k].wait()

    swap_end(2, 0, move_h)
    packed[0, 0, 0, 0, 0] = (pack(0) * norm_scale * gain[...].reshape(1, width)).astype(bf16)
    gather_first(0)
    swap_end(2, 1, move_c)
    packed[1, 0, 0, 0, 0] = (pack(1) * (grad_scale / 4.0)).astype(bf16)
    gather_first(1)
    gather_second(0)
    gather_second(1)
    for p in range(3):
        gather_third(0, p)
    for copy in weight_copies:
        copy.wait()
    core_copies = []
    for n, (buf, where) in enumerate(
        ((w_up, (slice(None), slice(None), own_units)), (w_dn, (slice(None), own_units)))
    ):
        copy = remote(buf.at[where], buf.at[where], core_send.at[n], core_recv.at[n], core)
        copy.start()
        core_copies.append(copy)
    for p in range(3):
        gather_pass_on(0, p)
        gather_third(1, p)
    for copy in core_copies:
        copy.wait()
    gather_end(0)

    tokens_here = 8 * CAP

    def streamed(buf, body):
        def fetch(j, slot):
            return pltpu.make_async_copy(buf.at[j // 2, j % 2], stream.at[slot], stream_sem.at[slot])

        fetch(0, 0).start()

        def turn(j, carry):
            slot = j % 2

            @pl.when(j < 7)
            def _():
                fetch(j + 1, 1 - slot).start()

            fetch(j, slot).wait()
            body(j, stream[slot].reshape(tokens_here, width))
            return carry

        lax.fori_loop(0, 8, turn, 0)

    acc[...] = jnp.zeros_like(acc)

    def forward(j, block):
        acc[...] += jnp.dot(block, w_up[j], preferred_element_type=f32)

    streamed(g_norm, forward)
    value = acc[...] / root_width
    sigma = 1.0 / (1.0 + jnp.exp(-value))
    slope[...] = sigma * (1.0 + value * (1.0 - sigma))
    hidden[...] = (value * sigma).astype(bf16)

    def down(j, carry):
        block = jnp.dot(hidden[...], w_dn[j], preferred_element_type=f32)
        part[j // 2, j % 2] = block.astype(bf16).reshape(4, 2, CAP, width)
        return carry

    lax.fori_loop(0, 8, down, 0)
    for p in range(3):
        gather_pass_on(1, p)

    sends = {}
    for p, (r0, nr) in enumerate(PARTS[2]):
        one, two, three = ORDERS[p]
        row = pl.ds(r0, nr)
        for k, step in enumerate((1, 3)):
            src = part.at[spans({one: (at[one] + 2) % 4, two: ("half", k), three: None}) + (row,)]
            sends[p, k] = remote(
                src, half_bufs[p].at[k], h_send.at[p, k], h_recv.at[p, k], shifted(at, one, step)
            )
            sends[p, k].start()
    for p, (r0, nr) in enumerate(PARTS[2]):
        one, two, three = ORDERS[p]
        row = pl.ds(r0, nr)
        for k, step in enumerate((1, 3)):
            other = 1 - k
            src = part.at[spans({one: (at[one] + step) % 4, two: ("half", other), three: None}) + (row,)]
            dst = full_bufs[p].at[(k,) + spans({one: 0, two: ("half", other), three: None})]
            sends[p, 2 + k] = remote(
                src, dst, f_send.at[p, k, 0], f_recv.at[p, k, 0], shifted(at, one, step)
            )
            sends[p, 2 + k].start()

    gather_end(1)
    acc[...] = jnp.zeros_like(acc)
    turned[...] = jnp.transpose(hidden[...])
    own_first = at["c"] == 0
    own_rows = pl.ds(pl.multiple_of(at["c"] * units, units), units)

    def give(buf, dst, send, recv, j):
        return remote(buf.at[j], dst.at[j], send.at[j], recv.at[j], core)

    def backward(j, block):
        acc[...] += lax.dot_general(block, w_dn[j], (((1,), (1,)), ((), ())), preferred_element_type=f32)
        grad = jnp.dot(turned[...], block, preferred_element_type=f32) * (step_size / root_units)
        low, high = grad[:units], grad[units:]
        own_dn[j] = w_dn[j, own_rows].astype(f32) - jnp.where(own_first, low, high)
        oth_dn[j] = jnp.where(own_first, high, low)
        give(oth_dn, got_dn, gd_send, gd_recv, j).start()

    streamed(g_out, backward)

    for p, (r0, nr) in enumerate(PARTS[2]):
        one, two, three = ORDERS[p]
        for k, step in enumerate((1, 3)):
            sends[p, k].wait()
            sel = {one: 0, two: ("half", k), three: None}
            dims = sizes(sel, nr, width)[:4]
            base = starts_of({one: (at[one] + step) % 4, two: ("half", k), three: None})

            def add(q, carry, p=p, k=k, dims=dims, base=base, r0=r0, nr=nr):
                ix = lead(q, dims)
                half_bufs[p][(k,) + ix] = (
                    half_bufs[p][(k,) + ix] + part[moved(base, ix) + (pl.ds(r0, nr),)]
                )
                return carry

            lax.fori_loop(0, count(dims), add, 0)
            dst = full_bufs[p].at[(k,) + spans(sel)]
            sends[p, 4 + k] = remote(
                half_bufs[p].at[k], dst, f_send.at[p, k, 1], f_recv.at[p, k, 1], shifted(at, one, step)
            )
            sends[p, 4 + k].start()

    turned[...] = jnp.transpose((acc[...] / root_units * slope[...]).astype(bf16))

    def up_grad(j, block):
        grad = jnp.dot(turned[...], block, preferred_element_type=f32) * (step_size / root_width)
        low, high = jnp.transpose(grad[:units]), jnp.transpose(grad[units:])
        weight = w_up[j].astype(f32)
        base = jnp.where(own_first, weight[:, :units], weight[:, units:])
        own_up[j] = base - jnp.where(own_first, low, high)
        oth_up[j] = jnp.where(own_first, high, low)
        give(oth_up, got_up, gu_send, gu_recv, j).start()

    streamed(g_norm, up_grad)

    def put_dn(j):
        return pltpu.make_async_copy(
            own_dn.at[j], new_dn.at[:, pl.ds(pl.multiple_of(j * width, 128), width)], nd_sem.at[j]
        )

    def put_up(j):
        return pltpu.make_async_copy(
            own_up.at[j], new_up.at[pl.ds(pl.multiple_of(j * width, 128), width)], nu_sem.at[j]
        )

    def finish_dn(j, carry):
        give(oth_dn, got_dn, gd_send, gd_recv, j).wait()
        own_dn[j] = own_dn[j] - got_dn[j]
        put_dn(j).start()
        return carry

    def finish_up(j, carry):
        give(oth_up, got_up, gu_send, gu_recv, j).wait()
        own_up[j] = own_up[j] - got_up[j]
        put_up(j).start()
        return carry

    lax.fori_loop(0, 8, finish_dn, 0)
    lax.fori_loop(0, 8, finish_up, 0)

    for p, (r0, nr) in enumerate(PARTS[2]):
        one, two, three = ORDERS[p]
        for n in (2, 3, 4, 5):
            sends[p, n].wait()
        for k, step in enumerate(OFFSETS + (0,)):
            spot = (at[two] + step) % 4
            dims = sizes({one: 0, two: 0, three: None}, nr, width)[:4]
            local = starts_of({one: 0, two: spot, three: None})
            base = starts_of({one: at[one], two: spot, three: None})

            def add(q, carry, p=p, dims=dims, local=local, base=base, r0=r0, nr=nr):
                ix = lead(q, dims)
                there = moved(local, ix)
                value = full_bufs[p][(0,) + there].astype(f32) + full_bufs[p][(1,) + there].astype(f32)
                value = value + part[moved(base, ix) + (pl.ds(r0, nr),)].astype(f32)
                full_bufs[p][(0,) + there] = value.astype(bf16)
                return carry

            lax.fori_loop(0, 4, add, 0)
            if step:
                src = full_bufs[p].at[(0,) + spans({one: 0, two: spot, three: None})]
                sends[p, 6 + k] = remote(
                    src, two_bufs[p].at[k], t_send.at[p, k], t_recv.at[p, k], shifted(at, two, step)
                )
                sends[p, 6 + k].start()
    for p, (r0, nr) in enumerate(PARTS[2]):
        one, two, three = ORDERS[p]
        for k in range(3):
            sends[p, 6 + k].wait()
        dims = sizes({one: 0, two: 0, three: None}, nr, width)[:4]
        local = starts_of({one: 0, two: at[two], three: None})
        for q in range(4):
            ix = lead(q, dims)
            value = full_bufs[p][(0,) + moved(local, ix)].astype(f32)
            for k in range(3):
                value = value + two_bufs[p][(k,) + ix].astype(f32)
            two_bufs[p][(0,) + ix] = value.astype(bf16)
        for k, step in enumerate(OFFSETS):
            src = two_bufs[p].at[(0,) + spans({one: 0, two: 0, three: (at[three] + step) % 4})]
            sends[p, 9 + k] = remote(
                src, one_bufs[p].at[k], o_send.at[p, k], o_recv.at[p, k], shifted(at, three, step)
            )
            sends[p, 9 + k].start()
    for p, (r0, nr) in enumerate(PARTS[2]):
        one, two, three = ORDERS[p]
        for k in range(3):
            sends[p, 9 + k].wait()
        there = starts_of({one: 0, two: 0, three: at[three]})
        value = two_bufs[p][(0,) + there].astype(f32)
        for k in range(3):
            value = value + one_bufs[p][k, 0, 0, 0, 0].astype(f32)
        tokens[pl.ds(r0, nr)] = (value / root_units).astype(bf16)
    for s in range(row_count):
        out[s] = lax.dot_general(
            masks[s], tokens[...], (((0,), (0,)), ((), ())), preferred_element_type=f32
        ).astype(bf16)

    def drain(j, carry):
        put_dn(j).wait()
        put_up(j).wait()
        return carry

    lax.fori_loop(0, 8, drain, 0)


def on_device(
    hidden_rows, cotangent, lengths, rewards, swap_rows, norm_gain, up_weight, down_weight
):
    row_count, slot_len, width = hidden_rows.shape
    root_width = math.sqrt(width * lax.axis_size("mp"))
    root_units = math.sqrt(up_weight.shape[1] * lax.axis_size("dp"))
    f32, bf16 = jnp.float32, jnp.bfloat16
    blocks = (4, 2, 4, 2, CAP, width)
    tokens = 8 * CAP
    dma = pltpu.SemaphoreType.DMA
    vmem = pl.BlockSpec(memory_space=pltpu.VMEM)
    smem = pl.BlockSpec(memory_space=pltpu.SMEM)
    hbm = pl.BlockSpec(memory_space=pl.ANY)
    half, full, two_b, one_b = [], [], [], []
    for (one, two, three), (_, nr) in zip(ORDERS, PARTS[2]):
        half.append(pltpu.VMEM((2,) + sizes({one: 0, two: ("half", 0), three: None}, nr, width), bf16))
        full.append(pltpu.VMEM((2,) + sizes({one: 0, two: None, three: None}, nr, width), bf16))
        two_b.append(pltpu.VMEM((3,) + sizes({one: 0, two: 0, three: None}, nr, width), bf16))
        one_b.append(pltpu.VMEM((3, 1, 1, 1, 1, nr, width), bf16))

    def body(*refs):
        step_kernel(root_width, root_units, *refs)

    block_out, new_up, new_dn, _, _ = pl.pallas_call(
        body,
        out_shape=(
            jax.ShapeDtypeStruct((row_count, slot_len, width), bf16),
            jax.ShapeDtypeStruct((8 * width, 128), f32),
            jax.ShapeDtypeStruct((128, 8 * width), f32),
            jax.ShapeDtypeStruct(blocks, bf16),
            jax.ShapeDtypeStruct(blocks, bf16),
        ),
        in_specs=[hbm, hbm, vmem, smem, smem, smem, hbm, hbm],
        out_specs=(vmem, hbm, hbm, hbm, hbm),
        scratch_shapes=[
            pltpu.VMEM((row_count, slot_len, width), bf16),
            pltpu.VMEM((row_count, slot_len, width), bf16),
            pltpu.VMEM((3, 2, 2, slot_len, width), bf16),
            pltpu.VMEM((3, 2, 2, slot_len, width), bf16),
            pltpu.VMEM((row_count, 8, 128), f32),
            pltpu.VMEM((3, 2, 8, 128), f32),
            pltpu.VMEM((3, 2, 8, 128), f32),
            pltpu.VMEM((8, 8, row_count * slot_len), f32),
            pltpu.VMEM((2, 1, 1, 1, 1, CAP, width), bf16),
            pltpu.VMEM((row_count, CAP, slot_len), bf16),
            pltpu.VMEM((8, width, 256), bf16),
            pltpu.VMEM((8, 256, width), bf16),
            pltpu.VMEM((2, 4, 2, CAP, width), bf16),
            pltpu.VMEM((tokens, 256), f32),
            pltpu.VMEM((tokens, 256), bf16),
            pltpu.VMEM((256, tokens), bf16),
            pltpu.VMEM((tokens, 256), f32),
            pltpu.VMEM(blocks, bf16),
            pltpu.VMEM((8, width, 128), f32),
            pltpu.VMEM((8, width, 128), f32),
            pltpu.VMEM((8, width, 128), f32),
            pltpu.VMEM((8, 128, width), f32),
            pltpu.VMEM((8, 128, width), f32),
            pltpu.VMEM((8, 128, width), f32),
            pltpu.VMEM((CAP, width), bf16),
        ] + half + full + two_b + one_b + [
            dma((7,)), dma((7,)), dma((3, 2)), dma((3, 2)), dma((3,)), dma((3,)),
            dma((7,)), dma((7,)), dma((7,)), dma((7,)), dma((6,)), dma((2,)), dma((2,)),
            dma((2, 3, 3)), dma((2, 3, 3)), dma((2, 3, 3)), dma((2, 3, 3)),
            dma((2, 3, 4)), dma((2, 3, 4)),
            dma((2,)), dma((8,)), dma((8,)), dma((8,)), dma((8,)), dma((8,)), dma((8,)),
            dma((3, 2)), dma((3, 2)), dma((3, 2, 2)), dma((3, 2, 2)),
            dma((3, 3)), dma((3, 3)), dma((3, 3)), dma((3, 3)),
        ],
        compiler_params=pltpu.CompilerParams(
            collective_id=1, has_side_effects=True, vmem_limit_bytes=60 << 20
        ),
        name="policy_step",
    )(
        hidden_rows, cotangent, norm_gain, lengths, rewards, swap_rows, up_weight, down_weight,
    )
    return (block_out, new_up, new_dn)


def solution(mesh):
    return jax.shard_map(
        on_device,
        mesh=mesh,
        in_specs=(
            P("dp", None, "mp"),
            P("dp", None, "mp"),
            P("dp"),
            P("dp"),
            P("dp", None, None),
            P("mp"),
            P("mp", "dp"),
            P("dp", "mp"),
        ),
        out_specs=(P("dp", None, "mp"), P(None, ("dp", "mp")), P(("dp", "mp"), None)),
        check_vma=False,
    )
```

time: 926 us -> 210 us (0.23)
  waiting for transfers between devices: 772 us -> 0 us
  Pallas kernels: 0 us -> 200 us
  matrix products: 38.1 us -> 0 us
  local copies, waits for them, and re-layouts: 34.5 us -> 8.11 us
  other arithmetic: 25.2 us -> 0 us
  starting transfers between devices: 22.1 us -> 0 us
  blocking collectives: 19.7 us -> 0 us
  between operations: 14.5 us -> 0.64 us
    psum x1 -> x0, waiting for transfers between devices: 333 us -> none  [on_device(): preact = lax.psum(partial_pre, 'mp') / root_width]
    reduce_scatter x2 -> x0, waiting for transfers between devices: 236 us -> none  [the longest x1 168 us: on_device(): lax.psum_scatter(back_partial, 'mp', scatter_dimension=0, tiled=True)]
    pallas_call x0 -> x1, Pallas kernels: none -> 200 us  [on_device(): pl.pallas_call(body, out_shape=(jax.ShapeDtypeStruct((row_count, slot_len...]
    all_gather x3 -> x0, waiting for transfers between devices: 189 us -> none  [the longest x1 97.2 us: on_device(): grad_pre = lax.all_gather(slope_share, 'mp', axis=0, tiled=True)]
    dot_general x5 -> x0, matrix products: 38.1 us -> none  [the longest x1 8.76 us: on_device(): jnp.dot(gathered, up_weight, preferred_element_type=jnp.float32)]
    psum x1 -> x0, blocking collectives: 19.7 us -> none  [on_device(): total_square = lax.psum(jnp.sum(as_float * as_float, axis=1), 'mp')]
    ppermute x6 -> x0, waiting for transfers between devices: 13.4 us -> none  [partner(): return lax.ppermute(block, axis, route)]
    ppermute x6 -> x0, starting transfers between devices: 11.4 us -> none  [partner(): return lax.ppermute(block, axis, route)]
  transfers between devices with their start and end apart: 14 -> 0, of which waited for: 10 -> 0; matrix products, arithmetic and copies ran while one was open for 8% -> 0% of each run, Pallas kernels for 0% -> 0%
where the time goes in v2:
time: 210 us; the launch traced here: 209 us
  Pallas kernels  200 us (95%)
  local copies, waits for them, and re-layouts  8.11 us (4%)
    pallas_call x1, Pallas kernels, on_device(): pl.pallas_call(body, out_shape=(jax.ShapeDtypeStruct((row_count, slot_len...  200 us
    unnamed x6, local copies, waits for them, and re-layouts  8.11 us

profile of v2, /device:TPU:0, one launch (start us, length us, event | category | flops | bytes accessed | tf_op | source)
XLA Modules:
  0.0 209.2 jit_solution(11172325834193233410)
XLA Ops:
  0.6 1.3 copy.11.refs_5_
  2.0 200.4 %policy_step.1 = (bf16[4,64,640]{2,1,0:T(8,128)(2,1)}, f32[5120,128]{1,0:T(8,128)}, f32[128,5120]{1,0:T(8,128)}, bf16[4,2,4,2,128,640]{5,4,3,2,1,0:T(8,128)(2,1)}, bf16[4,2,4,2,128,640]{5,4,3,2,1,0:T(8,128)(2,1)}) custom-call(bf16[4,64,640]{2,1,0:T(8,128)(2,1)} %refs_0_.1, bf16[4,64,640]{2,1,0:T(8,128)(2,1)} %refs_1_.1, f32[640]{0:T(1024)} %refs_2_.1, ...), custom_call_target="tpu_custom_call" | custom-call | tf_op jit(solution)/shard_map/policy_step/pallas_call | solution.py:589
  202.4 1.7 copy.15
  204.1 0.0 copy-start
  204.1 3.5 %copy.16 = f32[5120,128]{1,0:T(8,128)} copy(f32[5120,128]{1,0:T(8,128)} %get-tuple-element.13) | data formatting | bytes 5242880
  207.7 0.0 copy-done
  207.7 1.5 copy.17
Async XLA Ops:
  204.1 3.6 %copy-start = (f32[128,5120]{1,0:T(8,128)S(1)}, f32[128,5120]{1,0:T(8,128)}, u32[]{:S(2)}) copy-start(f32[128,5120]{1,0:T(8,128)} %get-tuple-element.14) | copy-start | bytes 7864324

commit v3 on v2

v3 whole, which is shorter than its diff:
```python
import math

import jax
import jax.numpy as jnp
from jax import lax
from jax.experimental import pallas as pl
from jax.experimental.pallas import tpu as pltpu
from jax.sharding import PartitionSpec as P

norm_eps = 1e-06
step_size = 4.0
MESH = pl.DeviceIdType.MESH

CAP = 128
ORDERS = (("x", "y", "z"), ("y", "z", "x"), ("z", "x", "y"))


def cut_block(last, *columns):
    chunks = []
    for c0, nc, rows in columns:
        r0 = 0
        for axis, nr in zip("xyz", rows):
            chunks.append((last[axis], r0, nr, c0, nc))
            r0 += nr
    return tuple(chunks)


GATHER_LAST = {"z": 0, "x": 1, "y": 2}
SCATTER_FIRST = {"x": 0, "y": 1, "z": 2}
PARTS = (
    cut_block(GATHER_LAST, (0, 640, (48, 48, 32))),
    cut_block(GATHER_LAST, (0, 640, (48, 32, 48))),
    cut_block(SCATTER_FIRST, (0, 384, (32, 48, 48)), (384, 256, (64, 32, 32))),
)
CHUNKS = len(PARTS[2])
MOST = max(len(chunks) for chunks in PARTS)
OFFSETS = (1, 3, 2)


def place():
    i = lax.axis_index("dp")
    j = lax.axis_index("mp")
    return {
        "x": i // 4,
        "y": j // 2,
        "z": ((i // 2) % 2) * 2 + j % 2,
        "c": i % 2,
    }


def device(at):
    z = at["z"]
    return ((at["x"] * 2 + z // 2) * 2 + at["c"], at["y"] * 2 + z % 2)


def shifted(at, axis, step):
    count = 2 if axis == "c" else 4
    return {**at, axis: (at[axis] + step) % count}


def spans(sel):
    def plain(s):
        if isinstance(s, tuple):
            return pl.ds(2 * s[1], 2)
        return pl.ds(0, 4) if s is None else pl.ds(s, 1)

    z = sel["z"]
    if z is None:
        z_lo, z_hi = pl.ds(0, 2), pl.ds(0, 2)
    elif isinstance(z, tuple):
        z_lo, z_hi = pl.ds(0, 2), pl.ds(z[1], 1)
    else:
        z_lo, z_hi = pl.ds(z % 2, 1), pl.ds(z // 2, 1)
    return (plain(sel["y"]), z_lo, plain(sel["x"]), z_hi)


def remote(src, dst, send, recv, at):
    return pltpu.make_async_remote_copy(
        src_ref=src,
        dst_ref=dst,
        send_sem=send,
        recv_sem=recv,
        device_id=device(at),
        device_id_type=MESH,
    )


def knock(peers):
    barrier = pltpu.get_barrier_semaphore()
    for at in peers:
        pl.semaphore_signal(barrier, inc=1, device_id=device(at), device_id_type=MESH)


def enter(peers):
    pl.semaphore_wait(pltpu.get_barrier_semaphore(), len(peers))


def axis_peers(at):
    return [shifted(at, axis, k) for axis in "xyz" for k in OFFSETS]


def row_mask(meta, slot, slot_len):
    length = meta[slot, 0:1, 0:1]
    start = jnp.zeros((1, 1), jnp.float32)
    for before in range(slot):
        start = start + meta[before, 0:1, 0:1]
    token = lax.broadcasted_iota(jnp.int32, (CAP, slot_len), 0).astype(jnp.float32)
    spot = lax.broadcasted_iota(jnp.int32, (CAP, slot_len), 1).astype(jnp.float32)
    return jnp.logical_and(token == spot + start, spot < length)


def sizes(sel, nr, width):
    def plain(s):
        return 2 if isinstance(s, tuple) else (4 if s is None else 1)

    z = sel["z"]
    z_dims = (2, 2) if z is None else ((2, 1) if isinstance(z, tuple) else (1, 1))
    return (plain(sel["y"]), z_dims[0], plain(sel["x"]), z_dims[1], nr, width)


def lead(q, dims):
    d = q % dims[3]
    q = q // dims[3]
    c = q % dims[2]
    q = q // dims[2]
    b = q % dims[1]
    return (q // dims[1], b, c, d)


def starts_of(sel):
    return tuple(s.start for s in spans(sel))


def moved(base, ix):
    return tuple(s + i for s, i in zip(base, ix))


def count(dims):
    return dims[0] * dims[1] * dims[2] * dims[3]


def unit_slope(preact):
    sigma = 1.0 / (1.0 + jnp.exp(-preact))
    return sigma * (1.0 + preact * (1.0 - sigma))


def step_kernel(
    root_width, root_units,
    hid, cot, gain_in, lens_in, rew_in, swp_in, up, dn,
    out, new_up, new_dn, g_norm, g_out,
    h_rows, c_rows, out_rows, in_rows, meta, out_meta, in_meta, squares, packed, masks,
    w_up, w_dn, stream, acc, hidden, turned, slope, part,
    own_up, oth_up, got_up, own_dn, oth_dn, got_dn, tokens,
    relay_up, relay_dn, gain, lens, rew, swp, *more
):
    half_bufs, full_bufs, two_bufs, one_bufs = (more[CHUNKS * n : CHUNKS * (n + 1)] for n in range(4))
    (
        sq_send, sq_recv, swap_send, swap_recv, meta_send, meta_recv,
        wy_send, wy_recv, wz_send, wz_recv, local_sem, core_send, core_recv,
        s1_send, s1_recv, s2_send, s2_recv, s3_send, s3_recv,
        stream_sem, gu_send, gu_recv, gd_send, gd_recv, nu_sem, nd_sem,
        h_send, h_recv, f_send, f_recv, t_send, t_recv, o_send, o_recv,
    ) = more[4 * CHUNKS :]
    at = place()
    row_count, slot_len, width = hid.shape
    units = 128
    f32, bf16 = jnp.float32, jnp.bfloat16

    loads = [
        pltpu.make_async_copy(src, dst, local_sem.at[4 + n])
        for n, (src, dst) in enumerate((
            (swp_in, swp), (hid, h_rows), (cot, c_rows), (lens_in, lens), (rew_in, rew), (gain_in, gain)
        ))
    ]
    for copy in loads:
        copy.start()
    mp_peers = [
        {**shifted(at, "y", dy), "z": (at["z"] // 2) * 2 + (at["z"] % 2 + dz) % 2}
        for dy in range(4) for dz in range(2) if dy or dz
    ]
    diagonal = [p for n, p in enumerate(mp_peers) if n in (2, 4, 6)]
    core = shifted(at, "c", 1)
    peers = axis_peers(at) + diagonal + [core]
    knock(peers)
    partners = (core, shifted(at, "z", 2), {**at, "x": (at["x"] // 2) * 2 + 1 - at["x"] % 2})

    store = (h_rows, c_rows)

    def swap_pick(r, a):
        out_rows[r, a, 0] = store[a][swp[0, r, 0]]
        out_rows[r, a, 1] = store[a][swp[0, r, 1]]

    def swap_start(r, a):
        if r:
            swap_pick(r, a)
        copy = remote(
            out_rows.at[r, a], in_rows.at[r, a], swap_send.at[r, a], swap_recv.at[r, a], partners[r]
        )
        copy.start()
        return copy

    def swap_end(r, a, copy):
        copy.wait()
        first, second = swp[0, r, 0], swp[0, r, 1]
        for s in range(row_count):
            store[a][s] = jnp.where(
                first == s, in_rows[r, a, 0], jnp.where(second == s, in_rows[r, a, 1], store[a][s])
            )

    def meta_start(r):
        out_meta[r, 0] = meta[swp[0, r, 0]]
        out_meta[r, 1] = meta[swp[0, r, 1]]
        copy = remote(out_meta.at[r], in_meta.at[r], meta_send.at[r], meta_recv.at[r], partners[r])
        copy.start()
        return copy

    def meta_end(r, copy):
        copy.wait()
        first, second = swp[0, r, 0], swp[0, r, 1]
        for s in range(row_count):
            meta[s] = jnp.where(first == s, in_meta[r, 0], jnp.where(second == s, in_meta[r, 1], meta[s]))

    def units_of(y, z_lo):
        return pl.ds(pl.multiple_of((y * 2 + z_lo) * units, units), units)

    z_lo = at["z"] % 2
    beside = {**at, "z": at["z"] + 1 - 2 * z_lo}
    own_units = pl.ds(pl.multiple_of(at["c"] * units, units), units)

    def weights_along_y():
        copies = {}
        for dy in (1, 3, 2):
            peer = shifted(at, "y", dy)
            near, far = units_of(peer["y"], z_lo), units_of(peer["y"], 1 - z_lo)
            moves = (
                (up.at[:, near], w_up.at[at["y"], z_lo, :, own_units]),
                (dn.at[near], w_dn.at[at["y"], z_lo, own_units]),
                (up.at[:, far], relay_up.at[at["y"]]),
                (dn.at[far], relay_dn.at[at["y"]]),
            )
            for n, (src, dst) in enumerate(moves):
                copy = remote(src, dst, wy_send.at[dy - 1, n], wy_recv.at[dy - 1, n], peer)
                copy.start()
                copies[dy, n] = copy
        near = units_of(at["y"], z_lo)
        for n, (src, dst) in enumerate(
            ((up.at[:, near], w_up.at[at["y"], z_lo, :, own_units]), (dn.at[near], w_dn.at[at["y"], z_lo, own_units]))
        ):
            copies[0, n] = pltpu.make_async_copy(src, dst, local_sem.at[n])
            copies[0, n].start()
        return copies

    def weights_along_z(dy):
        y = (at["y"] - dy) % 4
        far = units_of(y, 1 - z_lo)
        from_up = relay_up.at[y] if dy else up.at[:, far]
        from_dn = relay_dn.at[y] if dy else dn.at[far]
        copies = [
            remote(from_up, w_up.at[y, z_lo, :, own_units], wz_send.at[dy, 0], wz_recv.at[dy, 0], beside),
            remote(from_dn, w_dn.at[y, z_lo, own_units], wz_send.at[dy, 1], wz_recv.at[dy, 1], beside),
        ]
        for copy in copies:
            copy.start()
        return copies

    def weights_to_core(n, which):
        copies = [
            remote(
                w_up.at[:, which, :, own_units], w_up.at[:, which, :, own_units],
                core_send.at[n, 0], core_recv.at[n, 0], core,
            ),
            remote(
                w_dn.at[:, which, own_units], w_dn.at[:, which, own_units],
                core_send.at[n, 1], core_recv.at[n, 1], core,
            ),
        ]
        for copy in copies:
            copy.start()
        return copies

    for copy in loads:
        copy.wait()
    swap_pick(0, 0)
    swap_pick(0, 1)
    flat = h_rows[...].reshape(row_count * slot_len, width).astype(f32)
    squares[7] = lax.dot_general(
        jnp.ones((8, width), f32), flat * flat, (((1,), (1,)), ((), ())),
        precision=lax.Precision.HIGHEST, preferred_element_type=f32,
    )
    enter(peers)
    move_h = swap_start(0, 0)
    sq_copies = []
    for n, peer in enumerate(mp_peers):
        copy = remote(squares.at[7], squares.at[n], sq_send.at[n], sq_recv.at[n], peer)
        copy.start()
        sq_copies.append(copy)
    move_c = swap_start(0, 1)
    y_copies = weights_along_y()
    swap_end(0, 0, move_h)
    move_h = swap_start(1, 0)
    total = squares[7]
    for n, copy in enumerate(sq_copies):
        copy.wait()
        total = total + squares[n]
    factor = lax.rsqrt(total / (8 * width) + norm_eps)
    for s in range(row_count):
        meta[s, 0:1] = jnp.full((1, 128), lens[s].astype(f32), f32)
        meta[s, 1:2] = jnp.full((1, 128), rew[s].astype(f32), f32)
        meta[s, 2:8] = jnp.zeros((6, 128), f32)
        meta[s, 2:3, 0:slot_len] = factor[0:1, s * slot_len : (s + 1) * slot_len]
    move_m = meta_start(0)
    swap_end(0, 1, move_c)
    move_c = swap_start(1, 1)
    meta_end(0, move_m)
    move_m = meta_start(1)
    z_copies = weights_along_z(0)

    swap_end(1, 0, move_h)
    move_h = swap_start(2, 0)
    swap_end(1, 1, move_c)
    move_c = swap_start(2, 1)
    for dy in (1, 3):
        for n in (2, 3):
            y_copies[dy, n].wait()
        z_copies += weights_along_z(dy)
    meta_end(1, move_m)
    move_m = meta_start(2)
    meta_end(2, move_m)
    norm_scale = jnp.zeros((CAP, 1), f32)
    grad_scale = jnp.zeros((CAP, 1), f32)
    for s in range(row_count):
        hit = row_mask(meta, s, slot_len)
        masks[s] = jnp.where(hit, 1.0, 0.0).astype(bf16)
        norm_scale += jnp.sum(jnp.where(hit, meta[s, 2:3, 0:slot_len], 0.0), axis=1, keepdims=True)
        grad_scale += jnp.sum(jnp.where(hit, meta[s, 1:2, 0:slot_len], 0.0), axis=1, keepdims=True)

    def pack(a):
        picked = jnp.zeros((CAP, width), f32)
        for s in range(row_count):
            picked = picked + jnp.dot(masks[s], store[a][s], preferred_element_type=f32)
        return picked

    here = spans({k: at[k] for k in "xyz"})
    bufs = (g_norm, g_out)
    own, first_copies, second_copies, third_copies = [], {}, {}, {}

    def gather_first(a):
        copy = pltpu.make_async_copy(packed.at[a], bufs[a].at[here], local_sem.at[2 + a])
        copy.start()
        own.append(copy)
        for n, (p, r0, nr, c0, nc) in enumerate(PARTS[a]):
            for k, step in enumerate(OFFSETS):
                spot = (pl.ds(r0, nr), pl.ds(c0, nc))
                copy = remote(
                    packed.at[(a,) + (slice(None),) * 4 + spot], bufs[a].at[here + spot],
                    s1_send.at[a, n, k], s1_recv.at[a, n, k], shifted(at, ORDERS[p][0], step),
                )
                copy.start()
                first_copies[a, n, k] = copy

    def gather_second(a):
        own[a].wait()
        for n, (p, r0, nr, c0, nc) in enumerate(PARTS[a]):
            for k in range(3):
                first_copies[a, n, k].wait()
            one, two, three = ORDERS[p]
            spot = (pl.ds(r0, nr), pl.ds(c0, nc))
            piece = bufs[a].at[spans({one: None, two: at[two], three: at[three]}) + spot]
            for k, step in enumerate(OFFSETS):
                copy = remote(
                    piece, piece, s2_send.at[a, n, k], s2_recv.at[a, n, k], shifted(at, two, step)
                )
                copy.start()
                second_copies[a, n, k] = copy

    def gather_third(a, n):
        p, r0, nr, c0, nc = PARTS[a][n]
        for k in range(3):
            second_copies[a, n, k].wait()
        one, two, three = ORDERS[p]
        spot = (pl.ds(r0, nr), pl.ds(c0, nc))
        piece = bufs[a].at[spans({one: None, two: None, three: at[three]}) + spot]
        for k, step in enumerate((1, 3)):
            copy = remote(
                piece, piece, s3_send.at[a, n, k], s3_recv.at[a, n, k], shifted(at, three, step)
            )
            copy.start()
            third_copies[a, n, k] = copy

    def gather_pass_on(a, n):
        p, r0, nr, c0, nc = PARTS[a][n]
        one, two, three = ORDERS[p]
        spot = (pl.ds(r0, nr), pl.ds(c0, nc))
        for k, step in enumerate((1, 3)):
            third_copies[a, n, k].wait()
            origin = (at[three] - step) % 4
            piece = bufs[a].at[spans({one: ("half", k), two: None, three: origin}) + spot]
            copy = remote(
                piece, piece, s3_send.at[a, n, 2 + k], s3_recv.at[a, n, 2 + k], shifted(at, three, step)
            )
            copy.start()
            third_copies[a, n, 2 + k] = copy

    def gather_end(a):
        for n in range(len(PARTS[a])):
            for k in range(2):
                third_copies[a, n, 2 + k].wait()

    swap_end(2, 0, move_h)
    packed[0, 0, 0, 0, 0] = (pack(0) * norm_scale * gain[...].reshape(1, width)).astype(bf16)
    gather_first(0)
    swap_end(2, 1, move_c)
    packed[1, 0, 0, 0, 0] = (pack(1) * (grad_scale / 4.0)).astype(bf16)
    gather_first(1)
    gather_second(0)
    for n in (2, 3):
        y_copies[2, n].wait()
    z_copies += weights_along_z(2)
    gather_second(1)
    for n in range(len(PARTS[0])):
        gather_third(0, n)
    for dy in range(4):
        for n in range(2):
            y_copies[dy, n].wait()
    core_copies = weights_to_core(0, z_lo)
    for n in range(len(PARTS[0])):
        gather_pass_on(0, n)
    for n in range(len(PARTS[1])):
        gather_third(1, n)
    for copy in z_copies:
        copy.wait()
    core_copies += weights_to_core(1, 1 - z_lo)
    gather_end(0)
    for copy in core_copies:
        copy.wait()

    tokens_here = 8 * CAP

    def streamed(buf, body):
        def fetch(j, slot):
            return pltpu.make_async_copy(buf.at[j // 2, j % 2], stream.at[slot], stream_sem.at[slot])

        fetch(0, 0).start()

        def turn(j, carry):
            slot = j % 2

            @pl.when(j < 7)
            def _():
                fetch(j + 1, 1 - slot).start()

            fetch(j, slot).wait()
            body(j, stream[slot].reshape(tokens_here, width))
            return carry

        lax.fori_loop(0, 8, turn, 0)

    acc[...] = jnp.zeros_like(acc)

    def forward(j, block):
        acc[...] += jnp.dot(block, w_up[j // 2, j % 2], preferred_element_type=f32)

    streamed(g_norm, forward)
    value = acc[...] / root_width
    sigma = 1.0 / (1.0 + jnp.exp(-value))
    slope[...] = sigma * (1.0 + value * (1.0 - sigma))
    hidden[...] = (value * sigma).astype(bf16)

    def down(j, carry):
        block = jnp.dot(hidden[...], w_dn[j // 2, j % 2], preferred_element_type=f32)
        part[j // 2, j % 2] = block.astype(bf16).reshape(4, 2, CAP, width)
        return carry

    lax.fori_loop(0, 8, down, 0)
    for n in range(len(PARTS[1])):
        gather_pass_on(1, n)

    sends = {}
    for n, (p, r0, nr, c0, nc) in enumerate(PARTS[2]):
        one, two, three = ORDERS[p]
        spot = (pl.ds(r0, nr), pl.ds(c0, nc))
        for k, step in enumerate((1, 3)):
            src = part.at[spans({one: (at[one] + 2) % 4, two: ("half", k), three: None}) + spot]
            sends[n, k] = remote(
                src, half_bufs[n].at[k], h_send.at[n, k], h_recv.at[n, k], shifted(at, one, step)
            )
            sends[n, k].start()
    for n, (p, r0, nr, c0, nc) in enumerate(PARTS[2]):
        one, two, three = ORDERS[p]
        spot = (pl.ds(r0, nr), pl.ds(c0, nc))
        for k, step in enumerate((1, 3)):
            other = 1 - k
            src = part.at[spans({one: (at[one] + step) % 4, two: ("half", other), three: None}) + spot]
            dst = full_bufs[n].at[(k,) + spans({one: 0, two: ("half", other), three: None})]
            sends[n, 2 + k] = remote(
                src, dst, f_send.at[n, k, 0], f_recv.at[n, k, 0], shifted(at, one, step)
            )
            sends[n, 2 + k].start()

    gather_end(1)
    acc[...] = jnp.zeros_like(acc)
    turned[...] = jnp.transpose(hidden[...])
    own_first = at["c"] == 0
    own_rows = pl.ds(pl.multiple_of(at["c"] * units, units), units)

    def give(buf, dst, send, recv, j):
        return remote(buf.at[j], dst.at[j], send.at[j], recv.at[j], core)

    def backward(j, block):
        acc[...] += lax.dot_general(block, w_dn[j // 2, j % 2], (((1,), (1,)), ((), ())), preferred_element_type=f32)
        grad = jnp.dot(turned[...], block, preferred_element_type=f32) * (step_size / root_units)
        low, high = grad[:units], grad[units:]
        own_dn[j] = w_dn[j // 2, j % 2, own_rows].astype(f32) - jnp.where(own_first, low, high)
        oth_dn[j] = jnp.where(own_first, high, low)
        give(oth_dn, got_dn, gd_send, gd_recv, j).start()

    streamed(g_out, backward)

    for n, (p, r0, nr, c0, nc) in enumerate(PARTS[2]):
        one, two, three = ORDERS[p]
        spot = (pl.ds(r0, nr), pl.ds(c0, nc))
        for k, step in enumerate((1, 3)):
            sends[n, k].wait()
            sel = {one: 0, two: ("half", k), three: None}
            dims = sizes(sel, nr, nc)[:4]
            base = starts_of({one: (at[one] + step) % 4, two: ("half", k), three: None})

            def add(q, carry, n=n, k=k, dims=dims, base=base, spot=spot):
                ix = lead(q, dims)
                half_bufs[n][(k,) + ix] = half_bufs[n][(k,) + ix] + part[moved(base, ix) + spot]
                return carry

            lax.fori_loop(0, count(dims), add, 0)
            dst = full_bufs[n].at[(k,) + spans(sel)]
            sends[n, 4 + k] = remote(
                half_bufs[n].at[k], dst, f_send.at[n, k, 1], f_recv.at[n, k, 1], shifted(at, one, step)
            )
            sends[n, 4 + k].start()

    turned[...] = jnp.transpose((acc[...] / root_units * slope[...]).astype(bf16))

    def up_grad(j, block):
        grad = jnp.dot(turned[...], block, preferred_element_type=f32) * (step_size / root_width)
        low, high = jnp.transpose(grad[:units]), jnp.transpose(grad[units:])
        weight = w_up[j // 2, j % 2].astype(f32)
        base = jnp.where(own_first, weight[:, :units], weight[:, units:])
        own_up[j] = base - jnp.where(own_first, low, high)
        oth_up[j] = jnp.where(own_first, high, low)
        give(oth_up, got_up, gu_send, gu_recv, j).start()

    streamed(g_norm, up_grad)

    def put_dn(j):
        return pltpu.make_async_copy(
            own_dn.at[j], new_dn.at[:, pl.ds(pl.multiple_of(j * width, 128), width)], nd_sem.at[j]
        )

    def put_up(j):
        return pltpu.make_async_copy(
            own_up.at[j], new_up.at[pl.ds(pl.multiple_of(j * width, 128), width)], nu_sem.at[j]
        )

    def finish_dn(j, carry):
        give(oth_dn, got_dn, gd_send, gd_recv, j).wait()
        own_dn[j] = own_dn[j] - got_dn[j]
        put_dn(j).start()
        return carry

    def finish_up(j, carry):
        give(oth_up, got_up, gu_send, gu_recv, j).wait()
        own_up[j] = own_up[j] - got_up[j]
        put_up(j).start()
        return carry

    lax.fori_loop(0, 8, finish_dn, 0)
    lax.fori_loop(0, 8, finish_up, 0)

    for n, (p, r0, nr, c0, nc) in enumerate(PARTS[2]):
        one, two, three = ORDERS[p]
        spot = (pl.ds(r0, nr), pl.ds(c0, nc))
        for m in (2, 3, 4, 5):
            sends[n, m].wait()
        for k, step in enumerate(OFFSETS + (0,)):
            index = (at[two] + step) % 4
            dims = sizes({one: 0, two: 0, three: None}, nr, nc)[:4]
            local = starts_of({one: 0, two: index, three: None})
            base = starts_of({one: at[one], two: index, three: None})

            def add(q, carry, n=n, dims=dims, local=local, base=base, spot=spot):
                ix = lead(q, dims)
                there = moved(local, ix)
                value = full_bufs[n][(0,) + there].astype(f32) + full_bufs[n][(1,) + there].astype(f32)
                value = value + part[moved(base, ix) + spot].astype(f32)
                full_bufs[n][(0,) + there] = value.astype(bf16)
                return carry

            lax.fori_loop(0, 4, add, 0)
            if step:
                src = full_bufs[n].at[(0,) + spans({one: 0, two: index, three: None})]
                sends[n, 6 + k] = remote(
                    src, two_bufs[n].at[k], t_send.at[n, k], t_recv.at[n, k], shifted(at, two, step)
                )
                sends[n, 6 + k].start()
    for n, (p, r0, nr, c0, nc) in enumerate(PARTS[2]):
        one, two, three = ORDERS[p]
        for k in range(3):
            sends[n, 6 + k].wait()
        dims = sizes({one: 0, two: 0, three: None}, nr, nc)[:4]
        local = starts_of({one: 0, two: at[two], three: None})
        for q in range(4):
            ix = lead(q, dims)
            value = full_bufs[n][(0,) + moved(local, ix)].astype(f32)
            for k in range(3):
                value = value + two_bufs[n][(k,) + ix].astype(f32)
            two_bufs[n][(0,) + ix] = value.astype(bf16)
        for k, step in enumerate(OFFSETS):
            src = two_bufs[n].at[(0,) + spans({one: 0, two: 0, three: (at[three] + step) % 4})]
            sends[n, 9 + k] = remote(
                src, one_bufs[n].at[k], o_send.at[n, k], o_recv.at[n, k], shifted(at, three, step)
            )
            sends[n, 9 + k].start()
    for n, (p, r0, nr, c0, nc) in enumerate(PARTS[2]):
        one, two, three = ORDERS[p]
        for k in range(3):
            sends[n, 9 + k].wait()
        there = starts_of({one: 0, two: 0, three: at[three]})
        value = two_bufs[n][(0,) + there].astype(f32)
        for k in range(3):
            value = value + one_bufs[n][k, 0, 0, 0, 0].astype(f32)
        tokens[pl.ds(r0, nr), pl.ds(c0, nc)] = (value / root_units).astype(bf16)
    for s in range(row_count):
        out[s] = lax.dot_general(
            masks[s], tokens[...], (((0,), (0,)), ((), ())), preferred_element_type=f32
        ).astype(bf16)

    def drain(j, carry):
        put_dn(j).wait()
        put_up(j).wait()
        return carry

    lax.fori_loop(0, 8, drain, 0)


def on_device(
    hidden_rows, cotangent, lengths, rewards, swap_rows, norm_gain, up_weight, down_weight
):
    row_count, slot_len, width = hidden_rows.shape
    root_width = math.sqrt(width * lax.axis_size("mp"))
    root_units = math.sqrt(up_weight.shape[1] * lax.axis_size("dp"))
    f32, bf16 = jnp.float32, jnp.bfloat16
    blocks = (4, 2, 4, 2, CAP, width)
    tokens = 8 * CAP
    dma = pltpu.SemaphoreType.DMA
    vmem = pl.BlockSpec(memory_space=pltpu.VMEM)
    hbm = pl.BlockSpec(memory_space=pl.ANY)
    half, full, two_b, one_b = [], [], [], []
    for p, _, nr, _, nc in PARTS[2]:
        one, two, three = ORDERS[p]
        half.append(pltpu.VMEM((2,) + sizes({one: 0, two: ("half", 0), three: None}, nr, nc), bf16))
        full.append(pltpu.VMEM((2,) + sizes({one: 0, two: None, three: None}, nr, nc), bf16))
        two_b.append(pltpu.VMEM((3,) + sizes({one: 0, two: 0, three: None}, nr, nc), bf16))
        one_b.append(pltpu.VMEM((3, 1, 1, 1, 1, nr, nc), bf16))

    def body(*refs):
        step_kernel(root_width, root_units, *refs)

    block_out, new_up, new_dn, _, _ = pl.pallas_call(
        body,
        out_shape=(
            jax.ShapeDtypeStruct((row_count, slot_len, width), bf16),
            jax.ShapeDtypeStruct((8 * width, 128), f32),
            jax.ShapeDtypeStruct((128, 8 * width), f32),
            jax.ShapeDtypeStruct(blocks, bf16),
            jax.ShapeDtypeStruct(blocks, bf16),
        ),
        in_specs=[hbm] * 8,
        out_specs=(vmem, hbm, hbm, hbm, hbm),
        scratch_shapes=[
            pltpu.VMEM((row_count, slot_len, width), bf16),
            pltpu.VMEM((row_count, slot_len, width), bf16),
            pltpu.VMEM((3, 2, 2, slot_len, width), bf16),
            pltpu.VMEM((3, 2, 2, slot_len, width), bf16),
            pltpu.VMEM((row_count, 8, 128), f32),
            pltpu.VMEM((3, 2, 8, 128), f32),
            pltpu.VMEM((3, 2, 8, 128), f32),
            pltpu.VMEM((8, 8, row_count * slot_len), f32),
            pltpu.VMEM((2, 1, 1, 1, 1, CAP, width), bf16),
            pltpu.VMEM((row_count, CAP, slot_len), bf16),
            pltpu.VMEM((4, 2, width, 256), bf16),
            pltpu.VMEM((4, 2, 256, width), bf16),
            pltpu.VMEM((2, 4, 2, CAP, width), bf16),
            pltpu.VMEM((tokens, 256), f32),
            pltpu.VMEM((tokens, 256), bf16),
            pltpu.VMEM((256, tokens), bf16),
            pltpu.VMEM((tokens, 256), f32),
            pltpu.VMEM(blocks, bf16),
            pltpu.VMEM((8, width, 128), f32),
            pltpu.VMEM((8, width, 128), f32),
            pltpu.VMEM((8, width, 128), f32),
            pltpu.VMEM((8, 128, width), f32),
            pltpu.VMEM((8, 128, width), f32),
            pltpu.VMEM((8, 128, width), f32),
            pltpu.VMEM((CAP, width), bf16),
            pltpu.VMEM((4, width, 128), bf16),
            pltpu.VMEM((4, 128, width), bf16),
            pltpu.VMEM((width,), f32),
            pltpu.SMEM((row_count,), jnp.int32),
            pltpu.SMEM((row_count,), jnp.int32),
            pltpu.SMEM((1, 3, 2), jnp.int32),
        ] + half + full + two_b + one_b + [
            dma((7,)), dma((7,)), dma((3, 2)), dma((3, 2)), dma((3,)), dma((3,)),
            dma((3, 4)), dma((3, 4)), dma((4, 2)), dma((4, 2)), dma((10,)), dma((2, 2)), dma((2, 2)),
            dma((2, MOST, 3)), dma((2, MOST, 3)), dma((2, MOST, 3)), dma((2, MOST, 3)),
            dma((2, MOST, 4)), dma((2, MOST, 4)),
            dma((2,)), dma((8,)), dma((8,)), dma((8,)), dma((8,)), dma((8,)), dma((8,)),
            dma((CHUNKS, 2)), dma((CHUNKS, 2)), dma((CHUNKS, 2, 2)), dma((CHUNKS, 2, 2)),
            dma((CHUNKS, 3)), dma((CHUNKS, 3)), dma((CHUNKS, 3)), dma((CHUNKS, 3)),
        ],
        compiler_params=pltpu.CompilerParams(
            collective_id=1, has_side_effects=True, vmem_limit_bytes=60 << 20
        ),
        name="policy_step",
    )(
        hidden_rows, cotangent, norm_gain, lengths, rewards, swap_rows, up_weight, down_weight,
    )
    return (block_out, new_up, new_dn)


def solution(mesh):
    return jax.shard_map(
        on_device,
        mesh=mesh,
        in_specs=(
            P("dp", None, "mp"),
            P("dp", None, "mp"),
            P("dp"),
            P("dp"),
            P("dp", None, None),
            P("mp"),
            P("mp", "dp"),
            P("dp", "mp"),
        ),
        out_specs=(P("dp", None, "mp"), P(None, ("dp", "mp")), P(("dp", "mp"), None)),
        check_vma=False,
    )
```

time: 210 us -> 185 us (0.88)
  Pallas kernels: 200 us -> 176 us
    pallas_call x1, Pallas kernels: 200 us -> 176 us  [on_device(): pl.pallas_call(body, out_shape=(jax.ShapeDtypeStruct((row_count, slot_len...]
where the time goes in v3:
time: 185 us; the launch traced here: 184 us
  Pallas kernels  176 us (95%)
  local copies, waits for them, and re-layouts  8.11 us (4%)
    pallas_call x1, Pallas kernels, on_device(): pl.pallas_call(body, out_shape=(jax.ShapeDtypeStruct((row_count, slot_len...  176 us
    unnamed x6, local copies, waits for them, and re-layouts  8.11 us

profile of v3, /device:TPU:0, one launch (start us, length us, event | category | flops | bytes accessed | tf_op | source)
XLA Modules:
  0.0 184.3 jit_solution(2694798923520284221)
XLA Ops:
  0.6 1.3 copy.11.refs_5_
  2.0 175.5 %policy_step.1 = (bf16[4,64,640]{2,1,0:T(8,128)(2,1)}, f32[5120,128]{1,0:T(8,128)}, f32[128,5120]{1,0:T(8,128)}, bf16[4,2,4,2,128,640]{5,4,3,2,1,0:T(8,128)(2,1)}, bf16[4,2,4,2,128,640]{5,4,3,2,1,0:T(8,128)(2,1)}) custom-call(bf16[4,64,640]{2,1,0:T(8,128)(2,1)} %refs_0_.1, bf16[4,64,640]{2,1,0:T(8,128)(2,1)} %refs_1_.1, f32[640]{0:T(1024)} %refs_2_.1, ...), custom_call_target="tpu_custom_call" | custom-call | tf_op jit(solution)/shard_map/policy_step/pallas_call | solution.py:667
  177.5 1.7 copy.15
  179.2 0.0 copy-start
  179.2 3.5 %copy.16 = f32[5120,128]{1,0:T(8,128)} copy(f32[5120,128]{1,0:T(8,128)} %get-tuple-element.13) | data formatting | bytes 5242880
  182.8 0.0 copy-done
  182.8 1.5 copy.17
Async XLA Ops:
  179.2 3.6 %copy-start = (f32[128,5120]{1,0:T(8,128)S(1)}, f32[128,5120]{1,0:T(8,128)}, u32[]{:S(2)}) copy-start(f32[128,5120]{1,0:T(8,128)} %get-tuple-element.14) | copy-start | bytes 7864324

commit v4 on v3

--- a/solution.py
+++ b/solution.py
@@ -29,7 +29,7 @@
 SCATTER_FIRST = {"x": 0, "y": 1, "z": 2}
 PARTS = (
     cut_block(GATHER_LAST, (0, 640, (48, 48, 32))),
-    cut_block(GATHER_LAST, (0, 640, (48, 32, 48))),
+    cut_block(GATHER_LAST, (0, 384, (48, 32, 48)), (384, 256, (32, 48, 48))),
     cut_block(SCATTER_FIRST, (0, 384, (32, 48, 48)), (384, 256, (64, 32, 32))),
 )
 CHUNKS = len(PARTS[2])
@@ -151,7 +151,7 @@
     h_rows, c_rows, out_rows, in_rows, meta, out_meta, in_meta, squares, packed, masks,
     w_up, w_dn, stream, acc, hidden, turned, slope, part,
     own_up, oth_up, got_up, own_dn, oth_dn, got_dn, tokens,
-    relay_up, relay_dn, gain, lens, rew, swp, *more
+    relay_up, relay_dn, wide, gain, lens, rew, swp, *more
 ):
     half_bufs, full_bufs, two_bufs, one_bufs = (more[CHUNKS * n : CHUNKS * (n + 1)] for n in range(4))
     (
@@ -233,12 +233,12 @@
             peer = shifted(at, "y", dy)
             near, far = units_of(peer["y"], z_lo), units_of(peer["y"], 1 - z_lo)
             moves = (
-                (up.at[:, near], w_up.at[at["y"], z_lo, :, own_units]),
-                (dn.at[near], w_dn.at[at["y"], z_lo, own_units]),
-                (up.at[:, far], relay_up.at[at["y"]]),
-                (dn.at[far], relay_dn.at[at["y"]]),
-            )
-            for n, (src, dst) in enumerate(moves):
+                (2, up.at[:, far], relay_up.at[at["y"]]),
+                (3, dn.at[far], relay_dn.at[at["y"]]),
+                (0, up.at[:, near], w_up.at[at["y"], z_lo, :, own_units]),
+                (1, dn.at[near], w_dn.at[at["y"], z_lo, own_units]),
+            )
+            for n, src, dst in moves:
                 copy = remote(src, dst, wy_send.at[dy - 1, n], wy_recv.at[dy - 1, n], peer)
                 copy.start()
                 copies[dy, n] = copy
@@ -289,12 +289,12 @@
     )
     enter(peers)
     move_h = swap_start(0, 0)
+    move_c = swap_start(0, 1)
     sq_copies = []
     for n, peer in enumerate(mp_peers):
         copy = remote(squares.at[7], squares.at[n], sq_send.at[n], sq_recv.at[n], peer)
         copy.start()
         sq_copies.append(copy)
-    move_c = swap_start(0, 1)
     y_copies = weights_along_y()
     swap_end(0, 0, move_h)
     move_h = swap_start(1, 0)
@@ -310,21 +310,16 @@
         meta[s, 2:3, 0:slot_len] = factor[0:1, s * slot_len : (s + 1) * slot_len]
     move_m = meta_start(0)
     swap_end(0, 1, move_c)
-    move_c = swap_start(1, 1)
     meta_end(0, move_m)
     move_m = meta_start(1)
+    move_c = swap_start(1, 1)
     z_copies = weights_along_z(0)
-
     swap_end(1, 0, move_h)
     move_h = swap_start(2, 0)
+    meta_end(1, move_m)
+    move_m = meta_start(2)
     swap_end(1, 1, move_c)
     move_c = swap_start(2, 1)
-    for dy in (1, 3):
-        for n in (2, 3):
-            y_copies[dy, n].wait()
-        z_copies += weights_along_z(dy)
-    meta_end(1, move_m)
-    move_m = meta_start(2)
     meta_end(2, move_m)
     norm_scale = jnp.zeros((CAP, 1), f32)
     grad_scale = jnp.zeros((CAP, 1), f32)
@@ -412,6 +407,10 @@
     swap_end(2, 1, move_c)
     packed[1, 0, 0, 0, 0] = (pack(1) * (grad_scale / 4.0)).astype(bf16)
     gather_first(1)
+    for dy in (1, 3):
+        for n in (2, 3):
+            y_copies[dy, n].wait()
+        z_copies += weights_along_z(dy)
     gather_second(0)
     for n in (2, 3):
         y_copies[2, n].wait()
@@ -455,16 +454,37 @@
 
         lax.fori_loop(0, 8, turn, 0)
 
-    acc[...] = jnp.zeros_like(acc)
-
-    def forward(j, block):
-        acc[...] += jnp.dot(block, w_up[j // 2, j % 2], preferred_element_type=f32)
-
-    streamed(g_norm, forward)
-    value = acc[...] / root_width
-    sigma = 1.0 / (1.0 + jnp.exp(-value))
-    slope[...] = sigma * (1.0 + value * (1.0 - sigma))
-    hidden[...] = (value * sigma).astype(bf16)
+    rows_x = 2 * CAP
+
+    def fetch_x(x, slot):
+        return pltpu.make_async_copy(g_norm.at[:, :, x], wide.at[slot], stream_sem.at[slot])
+
+    fetch_x(0, 0).start()
+
+    def forward(x, carry):
+        slot = x % 2
+
+        @pl.when(x < 3)
+        def _():
+            fetch_x(x + 1, 1 - slot).start()
+
+        fetch_x(x, slot).wait()
+        value = jnp.zeros((rows_x, 256), f32)
+        for j in range(8):
+            value = value + jnp.dot(
+                wide[slot, j // 2, j % 2].reshape(rows_x, width), w_up[j // 2, j % 2],
+                preferred_element_type=f32,
+            )
+        value = value / root_width
+        sigma = 1.0 / (1.0 + jnp.exp(-value))
+        here_x = pl.ds(pl.multiple_of(x * rows_x, rows_x), rows_x)
+        slope[here_x] = sigma * (1.0 + value * (1.0 - sigma))
+        hidden[here_x] = (value * sigma).astype(bf16)
+        return carry
+
+    lax.fori_loop(0, 4, forward, 0)
+    for n in range(len(PARTS[1])):
+        gather_pass_on(1, n)
 
     def down(j, carry):
         block = jnp.dot(hidden[...], w_dn[j // 2, j % 2], preferred_element_type=f32)
@@ -472,8 +492,6 @@
         return carry
 
     lax.fori_loop(0, 8, down, 0)
-    for n in range(len(PARTS[1])):
-        gather_pass_on(1, n)
 
     sends = {}
     for n, (p, r0, nr, c0, nc) in enumerate(PARTS[2]):
@@ -703,6 +721,7 @@
             pltpu.VMEM((CAP, width), bf16),
             pltpu.VMEM((4, width, 128), bf16),
             pltpu.VMEM((4, 128, width), bf16),
+            pltpu.VMEM((2, 4, 2, 2, CAP, width), bf16),
             pltpu.VMEM((width,), f32),
             pltpu.SMEM((row_count,), jnp.int32),
             pltpu.SMEM((row_count,), jnp.int32),

time: 185 us -> 182 us (0.984)
  Pallas kernels: 176 us -> 173 us
    pallas_call x1, Pallas kernels: 176 us -> 173 us  [on_device(): pl.pallas_call(body, out_shape=(jax.ShapeDtypeStruct((row_count, slot_len...]
where the time goes in v4:
time: 182 us
  Pallas kernels  173 us (95%)
  local copies, waits for them, and re-layouts  8.11 us (4%)
    pallas_call x1, Pallas kernels, on_device(): pl.pallas_call(body, out_shape=(jax.ShapeDtypeStruct((row_count, slot_len...  173 us
    unnamed x6, local copies, waits for them, and re-layouts  8.11 us

profile of v4, /device:TPU:0, one launch (start us, length us, event | category | flops | bytes accessed | tf_op | source)
XLA Modules:
  0.0 181.9 jit_solution(10847414575540749542)
XLA Ops:
  0.6 1.3 copy.11.refs_5_
  2.0 173.1 %policy_step.1 = (bf16[4,64,640]{2,1,0:T(8,128)(2,1)}, f32[5120,128]{1,0:T(8,128)}, f32[128,5120]{1,0:T(8,128)}, bf16[4,2,4,2,128,640]{5,4,3,2,1,0:T(8,128)(2,1)}, bf16[4,2,4,2,128,640]{5,4,3,2,1,0:T(8,128)(2,1)}) custom-call(bf16[4,64,640]{2,1,0:T(8,128)(2,1)} %refs_0_.1, bf16[4,64,640]{2,1,0:T(8,128)(2,1)} %refs_1_.1, f32[640]{0:T(1024)} %refs_2_.1, ...), custom_call_target="tpu_custom_call" | custom-call | tf_op jit(solution)/shard_map/policy_step/pallas_call | solution.py:685
  175.1 1.7 copy.15
  176.8 0.0 copy-start
  176.8 3.5 %copy.16 = f32[5120,128]{1,0:T(8,128)} copy(f32[5120,128]{1,0:T(8,128)} %get-tuple-element.13) | data formatting | bytes 5242880
  180.4 0.0 copy-done
  180.4 1.5 copy.17
Async XLA Ops:
  176.8 3.6 %copy-start = (f32[128,5120]{1,0:T(8,128)S(1)}, f32[128,5120]{1,0:T(8,128)}, u32[]{:S(2)}) copy-start(f32[128,5120]{1,0:T(8,128)} %get-tuple-element.14) | copy-start | bytes 7864324

commit v5 on v4

--- a/solution.py
+++ b/solution.py
@@ -590,8 +590,6 @@
         put_up(j).start()
         return carry
 
-    lax.fori_loop(0, 8, finish_dn, 0)
-    lax.fori_loop(0, 8, finish_up, 0)
 
     for n, (p, r0, nr, c0, nc) in enumerate(PARTS[2]):
         one, two, three = ORDERS[p]
@@ -619,6 +617,8 @@
                     src, two_bufs[n].at[k], t_send.at[n, k], t_recv.at[n, k], shifted(at, two, step)
                 )
                 sends[n, 6 + k].start()
+    lax.fori_loop(0, 8, finish_dn, 0)
+    lax.fori_loop(0, 8, finish_up, 0)
     for n, (p, r0, nr, c0, nc) in enumerate(PARTS[2]):
         one, two, three = ORDERS[p]
         for k in range(3):

time: 182 us -> 183 us (level)
  no operation moved by 1% of the time
where the time goes in v5:
time: 183 us; the launch traced here: 182 us
  Pallas kernels  174 us (95%)
  local copies, waits for them, and re-layouts  8.11 us (4%)
    pallas_call x1, Pallas kernels, on_device(): pl.pallas_call(body, out_shape=(jax.ShapeDtypeStruct((row_count, slot_len...  174 us
    unnamed x6, local copies, waits for them, and re-layouts  8.11 us

profile of v5, /device:TPU:0, one launch (start us, length us, event | category | flops | bytes accessed | tf_op | source)
XLA Modules:
  0.0 182.5 jit_solution(14003818945933070802)
XLA Ops:
  0.6 1.3 copy.11.refs_5_
  2.0 173.7 %policy_step.1 = (bf16[4,64,640]{2,1,0:T(8,128)(2,1)}, f32[5120,128]{1,0:T(8,128)}, f32[128,5120]{1,0:T(8,128)}, bf16[4,2,4,2,128,640]{5,4,3,2,1,0:T(8,128)(2,1)}, bf16[4,2,4,2,128,640]{5,4,3,2,1,0:T(8,128)(2,1)}) custom-call(bf16[4,64,640]{2,1,0:T(8,128)(2,1)} %refs_0_.1, bf16[4,64,640]{2,1,0:T(8,128)(2,1)} %refs_1_.1, f32[640]{0:T(1024)} %refs_2_.1, ...), custom_call_target="tpu_custom_call" | custom-call | tf_op jit(solution)/shard_map/policy_step/pallas_call | solution.py:685
  175.7 1.7 copy.15
  177.4 0.0 copy-start
  177.4 3.5 %copy.16 = f32[5120,128]{1,0:T(8,128)} copy(f32[5120,128]{1,0:T(8,128)} %get-tuple-element.13) | data formatting | bytes 5242880
  181.0 0.0 copy-done
  181.0 1.5 copy.17
Async XLA Ops:
  177.4 3.6 %copy-start = (f32[128,5120]{1,0:T(8,128)S(1)}, f32[128,5120]{1,0:T(8,128)}, u32[]{:S(2)}) copy-start(f32[128,5120]{1,0:T(8,128)} %get-tuple-element.14) | copy-start | bytes 7864324
